TPU v7x, 256 devices: a whole 4x4x8 slice. The times are simulated.
256 devices in a mesh: band: 8 (over y, core), pw: 32 (over z, x).
Axes of the slice: x: 4, y: 4, z: 8, core: 2. Of those that a mesh axis runs over, the one named last changes fastest.
Arguments:
- orbitals: float32 [2, 8, 360, 4096], P(None, 'band', None, 'pw'), may hold values from -6 to 6
- response: float32 [2, 8, 360, 4096], P(None, 'band', None, 'pw'), may hold values from -6 to 6
- potential: float32 [32, 360, 360], P('pw'), may hold values from -8 to 8
- perturbation: float32 [32, 360, 360], P('pw'), may hold values from -6 to 6
- energies: float32 [8], P('band'), may hold values from -1 to 0
- stick_pos: int32 [4096], P('pw'), may hold values from 0 to 129599, as said below
Outputs:
- residual: float32 [2, 8, 360, 4096], P(None, 'band', None, 'pw')
- density: float32 [32, 360, 360], P('pw', 'band')
Inputs may be any that keep to these rules, and one draw needn't show every extreme that they name: `stick_pos`: the 4096 positions are all different; 0 and 129599 are among them.
All inputs are finite; a program needn't handle non-finite values.
Results may differ from a plain program's by a relative error of at most 0.0003.
Values sent between devices are 32-bit elements; how exact they have to be, the bound alone decides.
No kernel may reach another device: no remote copies, remote signals or barrier semaphores. Data moves between devices by JAX's collectives and lax.ppermute only.
A program may use at most 64 MiB of HBM per device.

v0:
```python
import functools
import math

import numpy as np
import jax
import jax.numpy as jnp
from jax import lax
from jax.experimental import pallas as pl
from jax.experimental.pallas import tpu as pltpu
from jax.sharding import PartitionSpec as P
import ml_dtypes

HIGHEST = lax.Precision.HIGHEST
F32 = jnp.float32
BF16 = jnp.bfloat16
GRID = 360
THIRD = 120
PAD = 384
SLOTS = 8
LANES = 128
WINDOW = 128
TALL = PAD + WINDOW
GROUP = 8
CHUNKS = LANES // GROUP
WIDE = 256
HALF_ROOT3 = math.sqrt(3.0) / 2.0
VMEM_LIMIT = 56 * 1024 * 1024


def trig(rows, cols):
    turns = (np.outer(rows, cols) % GRID) * (2.0 * math.pi / GRID)
    return np.cos(turns), np.sin(turns)


def split_table(table):
    high = table.astype(np.float32).astype(ml_dtypes.bfloat16)
    low = (table - high.astype(np.float64)).astype(ml_dtypes.bfloat16)
    return high, low


def transform_tables():
    small = np.arange(THIRD)
    spread = (small // 15) * 16 + small % 15

    def stack(sign, row_at, col_at, after_is_row):
        full = np.zeros((3 * 2 * LANES, 2 * LANES))
        for turn in range(3):
            after = 3 * small + turn
            if after_is_row:
                cos, sin = trig(after, small)
            else:
                cos, sin = trig(small, after)
            cos, sin = cos / math.sqrt(GRID), sin / math.sqrt(GRID)
            part = np.zeros((2 * LANES, 2 * LANES))
            part[np.ix_(row_at, col_at)] = cos
            part[np.ix_(row_at + LANES, col_at + LANES)] = cos
            part[np.ix_(row_at, col_at + LANES)] = sign * sin
            part[np.ix_(row_at + LANES, col_at)] = -sign * sin
            full[turn * 2 * LANES : (turn + 1) * 2 * LANES] = part
        return split_table(full)

    right = stack(1.0, small, small, False)
    left = stack(-1.0, spread, small, True)
    left_back = stack(1.0, small, spread, False)
    right_back = stack(-1.0, small, small, True)
    return right, left, left_back, right_back


def column_order():
    table = np.zeros((PAD, PAD), np.float32)
    points = np.arange(GRID)
    table[points, (points % 3) * LANES + points // 3] = 1.0
    return table.astype(ml_dtypes.bfloat16)


def halves(x):
    high = x.astype(BF16)
    return high, (x - high.astype(F32)).astype(BF16)


def dot(a, b):
    return jnp.dot(a, b, preferred_element_type=F32)


def dot3(a_high, a_low, b_high, b_low):
    return dot(a_high, b_high) + dot(a_low, b_high) + dot(a_high, b_low)


def three_point(a, b, c, sign):
    sums = [b[k] + c[k] for k in range(2)]
    mids = [a[k] - 0.5 * sums[k] for k in range(2)]
    diffs = [(sign * HALF_ROOT3) * (b[k] - c[k]) for k in range(2)]
    first = (a[0] + sums[0], a[1] + sums[1])
    second = (mids[0] - diffs[1], mids[1] + diffs[0])
    third = (mids[0] + diffs[1], mids[1] - diffs[0])
    return first, second, third


def sort_table(pos):
    across = jnp.broadcast_to(pos, (LANES, LANES))
    rank = jnp.sum(jnp.where(across.T < across, 1.0, 0.0), axis=0, keepdims=True)
    place = lax.broadcasted_iota(jnp.int32, (LANES, LANES), 0).astype(F32)
    return jnp.where(place == rank, 1.0, 0.0)


def exact_dot_t(values, table):
    return lax.dot_general(
        values, table, (((1,), (1,)), ((), ())), precision=HIGHEST, preferred_element_type=F32
    )


def planes_kernel(table_ref, orb_ref, chg_ref, pos_ref, out_ref):
    planes = table_ref.shape[0] // 2
    depth = table_ref.shape[1]
    both = jnp.concatenate(
        [orb_ref[...].reshape(depth, LANES), chg_ref[...].reshape(depth, LANES)], axis=1
    )
    pos = pos_ref[...].astype(F32)
    order = sort_table(pos)
    pos = exact_dot_t(jnp.broadcast_to(pos, (SLOTS, LANES)), order)[0:1, :]
    values = jnp.dot(table_ref[...], both, precision=HIGHEST, preferred_element_type=F32)
    values = exact_dot_t(
        jnp.concatenate([values[:, :LANES], values[:, LANES:]], axis=0), order
    )
    row = jnp.floor((pos + 0.5) * (1.0 / GRID))
    col = pos - row * GRID
    row = row + 8.0 * (jnp.where(row >= THIRD, 1.0, 0.0) + jnp.where(row >= 2 * THIRD, 1.0, 0.0))
    col = col + 8.0 * (jnp.where(col >= THIRD, 1.0, 0.0) + jnp.where(col >= 2 * THIRD, 1.0, 0.0))
    pieces = [values[k * planes : (k + 1) * planes] for k in range(4)] + [
        jnp.broadcast_to(row, (planes, LANES)),
        jnp.broadcast_to(col, (planes, LANES)),
        jnp.zeros((planes, LANES), F32),
        jnp.zeros((planes, LANES), F32),
    ]
    for slot, piece in enumerate(pieces):
        out_ref[pl.ds(slot, planes, stride=SLOTS), :] = piece


def reorder_kernel(pot_ref, per_ref, order_ref, out_ref, lines, rows):
    rows[...] = jnp.zeros_like(rows)
    lines[2 * GRID :, :] = jnp.zeros((GRID, LANES), F32)
    for field, ref in enumerate((pot_ref, per_ref)):
        for j in range(3):
            width = min(LANES, GRID - j * LANES)
            lines[j * GRID : (j + 1) * GRID, :width] = ref[0, :, j * LANES : j * LANES + width]
        for turn in range(3):
            for k in range(8):
                base = turn * LANES + 16 * k
                for j in range(3):
                    start = j * GRID + 45 * k + turn
                    rows[base : base + 15, j * LANES : (j + 1) * LANES] = lines[
                        pl.ds(start, 15, stride=3), :
                    ]
        high, low = halves(rows[...])
        out_ref[field] = dot(high, order_ref[...]) + dot(low, order_ref[...])


def exchange_lanes(blocks):
    group = lax.broadcasted_iota(jnp.int32, (SLOTS, LANES), 1) // GROUP
    blocks = list(blocks)
    for bit in range(4):
        step = 1 << bit
        high = (group & step) != 0
        for i in range(CHUNKS):
            if i & step:
                continue
            a, b = blocks[i], blocks[i + step]
            blocks[i] = jnp.where(high, pltpu.roll(b, GROUP * step, 1), a)
            blocks[i + step] = jnp.where(high, b, pltpu.roll(a, LANES - GROUP * step, 1))
    return blocks


def window_rows(vals, start):
    rows = lax.broadcasted_iota(jnp.int32, (WINDOW, WIDE), 0) + start
    return rows.astype(F32) == vals[4:5, :]


def column_hot(vals):
    cols = lax.broadcasted_iota(jnp.int32, (PAD, WIDE), 0).astype(F32)
    return jnp.where(cols == vals[5:6, :], 1.0, 0.0).astype(BF16)


def forward_kernel(
    vals_ref, pot_ref, rh_ref, rl_ref, lh_ref, ll_ref,
    keep_ref, send_ref, hh_ref, hl_ref, group_ref, win_ref,
    field, xh, xl, zh, zl, dens,
):
    core = lax.axis_index("band") % 2
    field[...] = jnp.zeros_like(field)
    for half in range(2):
        blocks = [
            vals_ref[(half * CHUNKS + j) * SLOTS : (half * CHUNKS + j + 1) * SLOTS, :]
            for j in range(CHUNKS)
        ]
        for q, block in enumerate(exchange_lanes(blocks)):
            group_ref[q * SLOTS : (q + 1) * SLOTS, half * LANES : (half + 1) * LANES] = block
    most = 0
    for q in range(CHUNKS):
        rows = group_ref[q * SLOTS + 4 : q * SLOTS + 5, :]
        low = jnp.min(rows).astype(jnp.int32)
        high = jnp.max(rows).astype(jnp.int32)
        start = jnp.bitwise_and(low, -16)
        count = lax.shift_right_logical(high - start, 7) + 1
        win_ref[q] = start
        win_ref[CHUNKS + q] = count
        most = jnp.maximum(most, count)
    win_ref[2 * CHUNKS] = most

    def place(q, start):
        vals = group_ref[pl.ds(pl.multiple_of(q * SLOTS, SLOTS), SLOTS), :]
        hot = jnp.where(window_rows(vals, start), 1.0, 0.0).astype(BF16)
        cols = column_hot(vals)
        scaled = []
        for comp in range(4):
            high, low = halves(vals[comp : comp + 1, :])
            scaled.append(jnp.concatenate([hot * high, hot * low], axis=1))
        placed = lax.dot_general(
            jnp.concatenate(scaled, axis=0),
            jnp.concatenate([cols, cols], axis=1),
            (((1,), (1,)), ((), ())),
            preferred_element_type=F32,
        )
        for comp in range(4):
            field[comp, pl.ds(start, WINDOW), :] += placed[comp * WINDOW : (comp + 1) * WINDOW]

    @pl.when(most == 1)
    def _():
        def four(step, _):
            for k in range(4):
                place(4 * step + k, pl.multiple_of(win_ref[4 * step + k], 16))
            return 0

        lax.fori_loop(0, CHUNKS // 4, four, 0)

    @pl.when(most > 1)
    def _():
        def one(q, _):
            def block(b, _):
                place(q, pl.multiple_of(win_ref[q] + b * WINDOW, 16))
                return 0

            lax.fori_loop(0, win_ref[CHUNKS + q], block, 0)
            return 0

        lax.fori_loop(0, CHUNKS, one, 0)

    step = 16
    for f in range(2):
        for r in range(0, LANES, step):
            rows = []
            for r2 in range(3):
                at = slice(r2 * LANES + r, r2 * LANES + r + step)
                cols = [
                    tuple(field[2 * f + k, at, c2 * LANES : (c2 + 1) * LANES] for k in range(2))
                    for c2 in range(3)
                ]
                rows.append(three_point(*cols, 1.0))
            for y2 in range(3):
                turned = three_point(rows[0][y2], rows[1][y2], rows[2][y2], 1.0)
                for x2 in range(3):
                    for k in range(2):
                        at = slice(f * PAD + x2 * LANES + r, f * PAD + x2 * LANES + r + step)
                        lanes = slice(y2 * WIDE + k * LANES, y2 * WIDE + (k + 1) * LANES)
                        high, low = halves(turned[x2][k])
                        xh[at, lanes] = high
                        xl[at, lanes] = low

    for y2 in range(3):
        at = slice(y2 * WIDE, (y2 + 1) * WIDE)
        out = dot3(xh[:, at], xl[:, at], rh_ref[at, :], rl_ref[at, :])
        for f in range(2):
            for x2 in range(3):
                for k in range(2):
                    part = out[
                        f * PAD + x2 * LANES : f * PAD + (x2 + 1) * LANES,
                        k * LANES : (k + 1) * LANES,
                    ]
                    rows = slice(x2 * WIDE + k * LANES, x2 * WIDE + (k + 1) * LANES)
                    lanes = slice(f * PAD + y2 * LANES, f * PAD + (y2 + 1) * LANES)
                    high, low = halves(part)
                    zh[rows, lanes] = high
                    zl[rows, lanes] = low

    for x2 in range(3):
        at = slice(x2 * WIDE, (x2 + 1) * WIDE)
        out = dot3(lh_ref[at, :], ll_ref[at, :], zh[at, :], zl[at, :])
        orb_r, chg_r = out[:LANES, :PAD], out[:LANES, PAD:]
        orb_i, chg_i = out[LANES:, :PAD], out[LANES:, PAD:]
        dens[x2] = 2.0 * (orb_r * chg_r + orb_i * chg_i)
        pot = pot_ref[0, x2 * LANES : (x2 + 1) * LANES, :]
        per = pot_ref[1, x2 * LANES : (x2 + 1) * LANES, :]
        for k, (chg, orb) in enumerate(((chg_r, orb_r), (chg_i, orb_i))):
            high, low = halves(pot * chg + per * orb)
            rows = slice(x2 * WIDE + k * LANES, x2 * WIDE + (k + 1) * LANES)
            hh_ref[rows, :] = high
            hl_ref[rows, :] = low
    for m in range(4):
        for x2 in range(3):
            own = pl.multiple_of(16 * (2 * m + core), 16)
            other = pl.multiple_of(16 * (2 * m + 1 - core), 16)
            keep_ref[m, 16 * x2 : 16 * (x2 + 1), :] = dens[x2, pl.ds(own, 16), :]
            send_ref[m, 16 * x2 : 16 * (x2 + 1), :] = dens[x2, pl.ds(other, 16), :]


def back_kernel(hh_ref, hl_ref, lh_ref, ll_ref, rh_ref, rl_ref, out_ref, mid, ph, plow):
    for x2 in range(3):
        at = slice(x2 * WIDE, (x2 + 1) * WIDE)
        mid[at, :] = dot3(lh_ref[at, :], ll_ref[at, :], hh_ref[at, :], hl_ref[at, :])
    step = 16
    for r in range(0, LANES, step):
        for y2 in range(3):
            lanes = slice(y2 * LANES, (y2 + 1) * LANES)
            parts = [
                tuple(
                    mid[x2 * WIDE + k * LANES + r : x2 * WIDE + k * LANES + r + step, lanes]
                    for k in range(2)
                )
                for x2 in range(3)
            ]
            for r2, pair in enumerate(three_point(*parts, -1.0)):
                for k in range(2):
                    high, low = halves(pair[k])
                    rows = slice(r2 * LANES + r, r2 * LANES + r + step)
                    to = slice(y2 * WIDE + k * LANES, y2 * WIDE + (k + 1) * LANES)
                    ph[rows, to] = high
                    plow[rows, to] = low
    for y2 in range(3):
        at = slice(y2 * WIDE, (y2 + 1) * WIDE)
        out = dot3(ph[:, at], plow[:, at], rh_ref[at, :], rl_ref[at, :])
        mid[:PAD, y2 * LANES : (y2 + 1) * LANES] = out[:, :LANES]
        mid[PAD:, y2 * LANES : (y2 + 1) * LANES] = out[:, LANES:]
    for r in range(0, PAD, step):
        parts = [
            tuple(
                mid[k * PAD + r : k * PAD + r + step, y2 * LANES : (y2 + 1) * LANES]
                for k in range(2)
            )
            for y2 in range(3)
        ]
        for q2, pair in enumerate(three_point(*parts, -1.0)):
            for k in range(2):
                high, low = halves(pair[k])
                out_ref[k, r : r + step, q2 * LANES : (q2 + 1) * LANES] = high
                out_ref[k, r : r + step, PAD + q2 * LANES : PAD + (q2 + 1) * LANES] = low
    out_ref[:, PAD:, :] = jnp.zeros((2, WINDOW, 2 * PAD), BF16)


def pick_kernel(grid_ref, group_ref, win_ref, keep_ref, got_ref, out_ref, *rest):
    block_refs, (picked, total) = rest[:4], rest[4:]
    chip = lax.axis_index("band") // 2
    total[...] = keep_ref[...] + got_ref[...]
    for k in range(4):
        block_refs[k][...] = total[jnp.bitwise_xor(chip, k)]

    def pick(q, start):
        vals = group_ref[pl.ds(pl.multiple_of(q * SLOTS, SLOTS), SLOTS), :]
        mask = window_rows(vals, start)
        cols = column_hot(vals)
        lines = grid_ref[:, pl.ds(start, WINDOW), :].reshape(2 * WINDOW, 2 * PAD)
        chosen = dot(lines, jnp.concatenate([cols, cols], axis=0))
        real = jnp.sum(jnp.where(mask, chosen[:WINDOW], 0.0), axis=0, keepdims=True)
        imag = jnp.sum(jnp.where(mask, chosen[WINDOW:], 0.0), axis=0, keepdims=True)
        return jnp.concatenate([real, imag, jnp.zeros((SLOTS - 2, WIDE), F32)], axis=0)

    most = win_ref[2 * CHUNKS]

    @pl.when(most == 1)
    def _():
        def four(step, _):
            for k in range(4):
                q = 4 * step + k
                at = pl.ds(pl.multiple_of(q * SLOTS, SLOTS), SLOTS)
                picked[at, :] = pick(q, pl.multiple_of(win_ref[q], 16))
            return 0

        lax.fori_loop(0, CHUNKS // 4, four, 0)

    @pl.when(most > 1)
    def _():
        picked[...] = jnp.zeros_like(picked)

        def one(q, _):
            at = pl.ds(pl.multiple_of(q * SLOTS, SLOTS), SLOTS)

            def block(b, _):
                picked[at, :] += pick(q, pl.multiple_of(win_ref[q] + b * WINDOW, 16))
                return 0

            lax.fori_loop(0, win_ref[CHUNKS + q], block, 0)
            return 0

        lax.fori_loop(0, CHUNKS, one, 0)

    for half in range(2):
        blocks = [
            picked[q * SLOTS : (q + 1) * SLOTS, half * LANES : (half + 1) * LANES]
            for q in range(CHUNKS)
        ]
        for j, block in enumerate(exchange_lanes(blocks)):
            src = half * CHUNKS + j
            out_ref[src * SLOTS : (src + 1) * SLOTS, :] = block


def residual_kernel(table_ref, order_ref, back_ref, chg_ref, pos_ref, energy_ref, *rest):
    parts = rest[:4]
    out_ref, dens_ref = rest[4:]
    planes = back_ref.shape[0] // SLOTS
    pos = pos_ref[...].astype(F32)
    order = sort_table(pos)
    real = back_ref[pl.ds(0, planes, stride=SLOTS), :]
    imag = back_ref[pl.ds(1, planes, stride=SLOTS), :]
    both = jnp.concatenate([real, imag], axis=0)
    both = jnp.dot(both, order, precision=HIGHEST, preferred_element_type=F32)
    applied = jnp.dot(table_ref[...], both, precision=HIGHEST, preferred_element_type=F32)
    row = jnp.floor((pos + 0.5) * (1.0 / GRID))
    col = pos - row * GRID
    half = GRID // 2
    row = jnp.where(row < half, row, row - GRID)
    col = jnp.where(col < half, col, col - GRID)
    depth = lax.broadcasted_iota(jnp.int32, (GRID, LANES), 0).astype(F32)
    depth = jnp.where(depth < half, depth, depth - GRID)
    kinetic = (depth * depth + (row * row + col * col)) * (8.0 / (GRID * GRID))
    factor = kinetic - energy_ref[0]
    out_ref[0, 0] = factor * chg_ref[0, 0] + applied[:GRID]
    out_ref[1, 0] = factor * chg_ref[1, 0] + applied[GRID:]
    high, low = halves(parts[0][...] + parts[1][...] + parts[2][...] + parts[3][...])
    turned = (((1,), (1,)), ((), ()))
    total = lax.dot_general(high, order_ref[...], turned, preferred_element_type=F32)
    total += lax.dot_general(low, order_ref[...], turned, preferred_element_type=F32)
    for i in range(15):
        for x2 in range(3):
            dens_ref[3 * i + x2] = total[16 * x2 + i : 16 * x2 + i + 1, :GRID]


def in_vmem(count):
    return [pl.BlockSpec(memory_space=pltpu.VMEM)] * count


def in_smem():
    return pl.BlockSpec(memory_space=pltpu.SMEM)


def call(kernel, name, outs, ins, out_specs, scratch=(), flops=0):
    return pl.pallas_call(
        kernel,
        out_shape=outs,
        in_specs=ins,
        out_specs=out_specs,
        scratch_shapes=list(scratch),
        compiler_params=pltpu.CompilerParams(vmem_limit_bytes=VMEM_LIMIT),
        cost_estimate=pl.CostEstimate(flops=flops, bytes_accessed=3_000_000, transcendentals=0),
        name=name,
    )


def shape(*dims, dtype=F32):
    return jax.ShapeDtypeStruct(dims, dtype)


def on_device(orbitals, response, potential, perturbation, energies, stick_pos):
    planes = lax.axis_size("pw")
    bands = lax.axis_size("band")
    cos, sin = trig(np.arange(planes), np.arange(GRID))
    to_planes = np.block([[cos, -sin], [sin, cos]]) / math.sqrt(GRID)
    from_planes = np.block([[cos.T, sin.T], [-sin.T, cos.T]]) / math.sqrt(planes)
    right, left, left_back, right_back = transform_tables()
    order = column_order()
    pos = stick_pos.reshape(1, LANES)

    packed = call(
        planes_kernel, "to_planes", shape(planes * SLOTS, LANES), in_vmem(4), in_vmem(1)[0],
        flops=500_000_000,
    )(to_planes.astype(np.float32), orbitals, response, pos)
    arrived = lax.all_to_all(
        packed.reshape(planes, SLOTS, LANES), "pw", split_axis=0, concat_axis=0, tiled=True
    ).reshape(planes * SLOTS, LANES)
    pots = call(
        reorder_kernel, "reorder", shape(2, PAD, PAD), in_vmem(3), in_vmem(1)[0],
        [pltpu.VMEM((3 * GRID, LANES), F32), pltpu.VMEM((PAD, PAD), F32)],
        flops=1_500_000_000,
    )(potential, perturbation, order)

    keep, send, h_high, h_low, group, windows = call(
        forward_kernel,
        "place_and_transform",
        [
            shape(4, 48, PAD),
            shape(4, 48, PAD),
            shape(2 * PAD, PAD, dtype=BF16),
            shape(2 * PAD, PAD, dtype=BF16),
            shape(CHUNKS * SLOTS, WIDE),
            shape(2 * CHUNKS + 1, dtype=jnp.int32),
        ],
        in_vmem(6),
        in_vmem(5) + [in_smem()],
        [
            pltpu.VMEM((4, TALL, PAD), F32),
            pltpu.VMEM((2 * PAD, 2 * PAD), BF16),
            pltpu.VMEM((2 * PAD, 2 * PAD), BF16),
            pltpu.VMEM((2 * PAD, 2 * PAD), BF16),
            pltpu.VMEM((2 * PAD, 2 * PAD), BF16),
            pltpu.VMEM((3, LANES, PAD), F32),
        ],
        flops=10_000_000_000,
    )(arrived, pots, *right, *left)
    got = lax.ppermute(send, "band", [(i, i ^ 1) for i in range(bands)])
    grid = call(
        back_kernel,
        "back",
        shape(2, TALL, 2 * PAD, dtype=BF16),
        in_vmem(6),
        in_vmem(1)[0],
        [
            pltpu.VMEM((2 * PAD, PAD), F32),
            pltpu.VMEM((PAD, 2 * PAD), BF16),
            pltpu.VMEM((PAD, 2 * PAD), BF16),
        ],
        flops=3_000_000_000,
    )(h_high, h_low, *left_back, *right_back)
    picked, *blocks = call(
        pick_kernel,
        "pick",
        [shape(planes * SLOTS, LANES)] + [shape(48, PAD)] * 4,
        in_vmem(2) + [in_smem()] + in_vmem(2),
        in_vmem(5),
        [pltpu.VMEM((CHUNKS * SLOTS, WIDE), F32), pltpu.VMEM((4, 48, PAD), F32)],
        flops=5_000_000_000,
    )(grid, group, windows, keep, got)
    returned = lax.all_to_all(
        picked.reshape(planes, SLOTS, LANES), "pw", split_axis=0, concat_axis=0, tiled=True
    ).reshape(planes * SLOTS, LANES)
    parts = [blocks[0]] + [
        lax.ppermute(blocks[k], "band", [(i, i ^ (2 * k)) for i in range(bands)])
        for k in range(1, 4)
    ]

    residual, density = call(
        residual_kernel,
        "from_planes",
        [shape(2, 1, GRID, LANES), shape(GRID // bands, 1, GRID)],
        in_vmem(5) + [in_smem()] + in_vmem(4),
        in_vmem(2),
        flops=500_000_000,
    )(from_planes.astype(np.float32), order, returned, response, pos, energies, *parts)
    return (residual, density.reshape(1, GRID // bands, GRID))


def solution(mesh):
    placed = (
        P(None, "band", None, "pw"),
        P(None, "band", None, "pw"),
        P("pw", None, None),
        P("pw", None, None),
        P("band"),
        P("pw"),
    )
    return jax.shard_map(
        on_device,
        mesh=mesh,
        in_specs=placed,
        out_specs=(P(None, "band", None, "pw"), P("pw", "band", None)),
        check_vma=False,
    )
```

profile of v0, /device:TPU:1, one launch (start us, length us, event | category | flops | bytes accessed | tf_op | source)
XLA Modules:
  0.0 67.7 jit_solution(7682046197675902047)
XLA Ops:
  0.6 2.8 %to_planes.1 = f32[256,128]{1,0:T(8,128)} custom-call(f32[64,720]{1,0:T(8,128)} %constant.22.clone.table_ref, f32[2,1,360,128]{3,2,1,0:T(8,128)} %orb_ref.1, f32[2,1,360,128]{3,2,1,0:T(8,128)} %chg_ref.3, s32[1,128]{1,0:T(1,128)} %bitcast.10), custom_call_target="tpu_custom_call" | custom-call | flops 500000000 | bytes 3000000 | tf_op jit(solution)/shard_map/to_planes/pallas_call | solution.py:470
  3.4 11.9 %all-to-all-start = ((f32[32,8,128]{2,1,0:T(8,128)}), f32[32,8,128]{2,1,0:T(8,128)S(1)}, u32[]{:S(2)}, u32[]{:S(2)}) async-start(f32[32,8,128]{2,1,0:T(8,128)} %bitcast.9), calls=%async_computation | async-start | bytes 262144 | tf_op jit(solution)/shard_map/all_to_all | solution.py:474
  15.3 3.3 %reorder.1.pot_ref = f32[2,384,384]{2,1,0:T(8,128)} custom-call(f32[1,360,360]{2,1,0:T(8,128)} %pot_ref.1, f32[1,360,360]{2,1,0:T(8,128)} %per_ref.1, bf16[384,384]{1,0:T(8,128)(2,1)} %constant.23.clone.order_ref), custom_call_target="tpu_custom_call" | custom-call | flops 1500000000 | bytes 3000000 | tf_op jit(solution)/shard_map/reorder/pallas_call | solution.py:477
  18.6 6.0 %all-to-all-done = f32[32,8,128]{2,1,0:T(8,128)S(1)} async-done(((f32[32,8,128]{2,1,0:T(8,128)}), f32[32,8,128]{2,1,0:T(8,128)S(1)}, u32[]{:S(2)}, u32[]{:S(2)}) %all-to-all-start) | async-done | bytes 131104 | tf_op jit(solution)/shard_map/all_to_all | solution.py:474
  24.7 0.7 copy-done.1
  25.3 12.5 %place_and_transform.1 = (f32[4,48,384]{2,1,0:T(8,128)}, f32[4,48,384]{2,1,0:T(8,128)}, bf16[768,384]{1,0:T(8,128)(2,1)}, bf16[768,384]{1,0:T(8,128)(2,1)}, f32[128,256]{1,0:T(8,128)}, /*index=5*/s32[33]{0:T(128)}) custom-call(f32[256,128]{1,0:T(8,128)} %bitcast.8, f32[2,384,384]{2,1,0:T(8,128)} %reorder.1.pot_ref, bf16[768,256]{1,0:T(8,128)(2,1)} %constant.24.clone.rh_ref, ...), custom_call_target="tpu_custom_call" | custom-call | flops 10000000000 | bytes 3000000 | tf_op jit(solution)/shard_map/place_and_transform/pallas_call | solution.py:483
  37.8 2.1 %collective-permute-start = (f32[4,48,384]{2,1,0:T(8,128)}, f32[4,48,384]{2,1,0:T(8,128)S(1)}, u32[]{:S(2)}, u32[]{:S(2)}) collective-permute-start(f32[4,48,384]{2,1,0:T(8,128)} %get-tuple-element.20), channel_id=1, source_target_pairs={{0,32},{32,0},{64,96},{96,64},{128,160},{160,128},{192,224},{224,1... | collective-permute-start | bytes 884744 | tf_op jit(solution)/shard_map/ppermute | solution.py:506
  39.9 4.6 %back.1.grid_ref = bf16[2,512,768]{2,1,0:T(8,128)(2,1)} custom-call(bf16[768,384]{1,0:T(8,128)(2,1)} %get-tuple-element.15.hh_ref, bf16[768,384]{1,0:T(8,128)(2,1)} %get-tuple-element.16.hl_ref, bf16[768,256]{1,0:T(8,128)(2,1)} %constant.28.clone.lh_ref, bf16[768,256]{1,0:T(8,128)(2,1)} %constant.29.clone.ll_ref, bf16[768,256]{1,0:T(8,128)(2,1)} %constant.30.clone.rh_ref, ...), custom_call_target="tpu_custom_call" | custom-call | flops 3000000000 | bytes 3000000 | tf_op jit(solution)/shard_map/back/pallas_call | solution.py:507
  44.5 0.0 collective-permute-done.got_ref
  44.5 0.7 %copy-done.2 = f32[4,48,384]{2,1,0:T(8,128)} copy-done((f32[4,48,384]{2,1,0:T(8,128)}, f32[4,48,384]{2,1,0:T(8,128)S(1)}, u32[]{:S(2)}) %copy-start.2) | copy-done | bytes 294936
  45.2 5.2 %pick.1 = (f32[256,128]{1,0:T(8,128)}, f32[48,384]{1,0:T(8,128)}, f32[48,384]{1,0:T(8,128)}, f32[48,384]{1,0:T(8,128)}, f32[48,384]{1,0:T(8,128)}) custom-call(bf16[2,512,768]{2,1,0:T(8,128)(2,1)} %back.1.grid_ref, f32[128,256]{1,0:T(8,128)} %get-tuple-element.17.group_ref, s32[33]{0:T(128)} %get-tuple-element.18.win_ref, ...), custom_call_target="tpu_custom_call" | custom-call | flops 5000000000 | bytes 3000000 | tf_op jit(solution)/shard_map/pick/pallas_call | solution.py:520
  50.4 3.8 %all-to-all-start.1 = ((f32[32,8,128]{2,1,0:T(8,128)}), f32[32,8,128]{2,1,0:T(8,128)S(1)}, u32[]{:S(2)}, u32[]{:S(2)}) async-start(f32[32,8,128]{2,1,0:T(8,128)} %bitcast.7), calls=%async_computation.1 | async-start | bytes 262144 | tf_op jit(solution)/shard_map/all_to_all | solution.py:529
  54.2 1.4 %collective-permute-start.1 = (f32[48,384]{1,0:T(8,128)}, f32[48,384]{1,0:T(8,128)S(1)}, u32[]{:S(2)}, u32[]{:S(2)}) collective-permute-start(f32[48,384]{1,0:T(8,128)} %get-tuple-element.23), channel_id=1, source_target_pairs={{0,64},{32,96},{64,0},{96,32},{128,192},{160,224},{192,128},{224,1... | collective-permute-start | bytes 221192 | tf_op jit(solution)/shard_map/ppermute | solution.py:533
  55.6 2.6 %collective-permute-start.2 = (f32[48,384]{1,0:T(8,128)}, f32[48,384]{1,0:T(8,128)S(1)}, u32[]{:S(2)}, u32[]{:S(2)}) collective-permute-start(f32[48,384]{1,0:T(8,128)} %get-tuple-element.24), channel_id=1, source_target_pairs={{0,128},{32,160},{64,192},{96,224},{128,0},{160,32},{192,64},{224,... | collective-permute-start | bytes 221192 | tf_op jit(solution)/shard_map/ppermute | solution.py:533
  58.2 0.0 collective-permute-start.3
  58.9 0.0 collective-permute-done.1.rest_1_
  58.9 0.0 copy-start.3
  58.9 3.5 %collective-permute-done.2.rest_2_ = f32[48,384]{1,0:T(8,128)S(1)} collective-permute-done((f32[48,384]{1,0:T(8,128)}, f32[48,384]{1,0:T(8,128)S(1)}, u32[]{:S(2)}, u32[]{:S(2)}) %collective-permute-start.2) | collective-permute-done | bytes 73760 | tf_op jit(solution)/shard_map/ppermute | solution.py:533
  62.4 1.4 %collective-permute-done.3.rest_3_ = f32[48,384]{1,0:T(8,128)S(1)} collective-permute-done((f32[48,384]{1,0:T(8,128)}, f32[48,384]{1,0:T(8,128)S(1)}, u32[]{:S(2)}, u32[]{:S(2)}) %collective-permute-start.3) | collective-permute-done | bytes 73760 | tf_op jit(solution)/shard_map/ppermute | solution.py:533
  63.8 0.2 all-to-all-done.1
  64.1 0.0 copy-done.4
  64.1 0.4 copy-done.5
  64.5 0.3 copy-done
  64.7 3.0 %from_planes.1 = (f32[2,1,360,128]{3,2,1,0:T(8,128)}, f32[45,1,360]{2,1,0:T(1,128)}) custom-call(f32[720,64]{1,0:T(8,128)} %constant.32.clone.table_ref, bf16[384,384]{1,0:T(8,128)(2,1)} %constant.23.clone.order_ref, f32[256,128]{1,0:T(8,128)} %bitcast.6, f32[2,1,360,128]{3,2,1,0:T(8,128)} %chg_ref.3, s32[1,128]{1,0:T(1,128)} %bitcast.11, ...), custom_call_target="tpu_custom_call" | custom-call | flops 500000000 | bytes 3000000 | tf_op jit(solution)/shard_map/from_planes/pallas_call | solution.py:537
  (6 shorter events, 0.0 us)
Async XLA Ops:
  3.4 21.2 %all-to-all-start = ((f32[32,8,128]{2,1,0:T(8,128)}), f32[32,8,128]{2,1,0:T(8,128)S(1)}, u32[]{:S(2)}, u32[]{:S(2)}) async-start(f32[32,8,128]{2,1,0:T(8,128)} %bitcast.9), calls=%async_computation | async-start | bytes 262144 | tf_op jit(solution)/shard_map/all_to_all | solution.py:474
  24.7 0.7 copy-start.1
  37.8 6.7 %collective-permute-start = (f32[4,48,384]{2,1,0:T(8,128)}, f32[4,48,384]{2,1,0:T(8,128)S(1)}, u32[]{:S(2)}, u32[]{:S(2)}) collective-permute-start(f32[4,48,384]{2,1,0:T(8,128)} %get-tuple-element.20), channel_id=1, source_target_pairs={{0,32},{32,0},{64,96},{96,64},{128,160},{160,128},{192,224},{224,1... | collective-permute-start | bytes 884744 | tf_op jit(solution)/shard_map/ppermute | solution.py:506
  44.5 0.7 %copy-start.2 = (f32[4,48,384]{2,1,0:T(8,128)}, f32[4,48,384]{2,1,0:T(8,128)S(1)}, u32[]{:S(2)}) copy-start(f32[4,48,384]{2,1,0:T(8,128)S(1)} %collective-permute-done.got_ref) | copy-start | bytes 884740
  50.4 13.7 %all-to-all-start.1 = ((f32[32,8,128]{2,1,0:T(8,128)}), f32[32,8,128]{2,1,0:T(8,128)S(1)}, u32[]{:S(2)}, u32[]{:S(2)}) async-start(f32[32,8,128]{2,1,0:T(8,128)} %bitcast.7), calls=%async_computation.1 | async-start | bytes 262144 | tf_op jit(solution)/shard_map/all_to_all | solution.py:529
  54.2 4.7 %collective-permute-start.1 = (f32[48,384]{1,0:T(8,128)}, f32[48,384]{1,0:T(8,128)S(1)}, u32[]{:S(2)}, u32[]{:S(2)}) collective-permute-start(f32[48,384]{1,0:T(8,128)} %get-tuple-element.23), channel_id=1, source_target_pairs={{0,64},{32,96},{64,0},{96,32},{128,192},{160,224},{192,128},{224,1... | collective-permute-start | bytes 221192 | tf_op jit(solution)/shard_map/ppermute | solution.py:533
  55.6 6.8 %collective-permute-start.2 = (f32[48,384]{1,0:T(8,128)}, f32[48,384]{1,0:T(8,128)S(1)}, u32[]{:S(2)}, u32[]{:S(2)}) collective-permute-start(f32[48,384]{1,0:T(8,128)} %get-tuple-element.24), channel_id=1, source_target_pairs={{0,128},{32,160},{64,192},{96,224},{128,0},{160,32},{192,64},{224,... | collective-permute-start | bytes 221192 | tf_op jit(solution)/shard_map/ppermute | solution.py:533
  58.2 5.6 %collective-permute-start.3 = (f32[48,384]{1,0:T(8,128)}, f32[48,384]{1,0:T(8,128)S(1)}, u32[]{:S(2)}, u32[]{:S(2)}) collective-permute-start(f32[48,384]{1,0:T(8,128)} %get-tuple-element.25), channel_id=1, source_target_pairs={{0,192},{32,224},{64,128},{96,160},{128,64},{160,96},{192,0},{224,... | collective-permute-start | bytes 221192 | tf_op jit(solution)/shard_map/ppermute | solution.py:533
  58.9 5.2 %copy-start.3 = (f32[48,384]{1,0:T(8,128)}, f32[48,384]{1,0:T(8,128)S(1)}, u32[]{:S(2)}) copy-start(f32[48,384]{1,0:T(8,128)S(1)} %collective-permute-done.1.rest_1_) | copy-start | bytes 221188
  62.4 1.7 %copy-start.4 = (f32[48,384]{1,0:T(8,128)}, f32[48,384]{1,0:T(8,128)S(1)}, u32[]{:S(2)}) copy-start(f32[48,384]{1,0:T(8,128)S(1)} %collective-permute-done.2.rest_2_) | copy-start | bytes 221188
  63.8 0.6 copy-start.5
  64.1 0.7 copy-start
where the time goes:
time: 68.2 us; the launch traced here: 67.7 us
  Pallas kernels  31.3 us (46%)
  starting transfers between devices  21.9 us (32%)
  waiting for transfers between devices  11.2 us (16%)
  local copies, waits for them, and re-layouts  2.03 us (3%)
  between operations  1.33 us (2%)
    pallas_call x1, Pallas kernels, on_device(): call(forward_kernel, 'place_and_transform', [shape(4, 48, PAD), shape(4,...  12.5 us
    all_to_all x1, starting transfers between devices, on_device(): lax.all_to_all(packed.reshape(planes, SLOTS, LANES), 'pw', split_axis=0,...  11.9 us
    all_to_all x1, waiting for transfers between devices, on_device(): lax.all_to_all(packed.reshape(planes, SLOTS, LANES), 'pw', split_axis=0,...  6.03 us
    pallas_call x1, Pallas kernels, on_device(): call(pick_kernel, 'pick', [shape(planes * SLOTS, LANES)] + [shape(48, PAD...  5.15 us
    ppermute x3, waiting for transfers between devices, on_device(): lax.ppermute(blocks[k], 'band', [(i, i ^ 2 * k) for i in range(bands)])  4.94 us
    pallas_call x1, Pallas kernels, on_device(): call(back_kernel, 'back', shape(2, TALL, 2 * PAD, dtype=BF16), in_vmem(6)...  4.57 us
    ppermute x3, starting transfers between devices, on_device(): lax.ppermute(blocks[k], 'band', [(i, i ^ 2 * k) for i in range(bands)])  4.01 us
    all_to_all x1, starting transfers between devices, on_device(): lax.all_to_all(picked.reshape(planes, SLOTS, LANES), 'pw', split_axis=0,...  3.84 us
  transfers between devices with their start and end apart: 6, of which 4 were waited for; matrix products, arithmetic and copies ran while one was open for 0% of the time, Pallas kernels for 12%

commit v1 on v0

--- a/solution.py
+++ b/solution.py
@@ -10,7 +10,6 @@
 from jax.sharding import PartitionSpec as P
 import ml_dtypes
 
-HIGHEST = lax.Precision.HIGHEST
 F32 = jnp.float32
 BF16 = jnp.bfloat16
 GRID = 360
@@ -24,7 +23,6 @@
 CHUNKS = LANES // GROUP
 WIDE = 256
 HALF_ROOT3 = math.sqrt(3.0) / 2.0
-VMEM_LIMIT = 56 * 1024 * 1024
 
 
 def trig(rows, cols):
@@ -103,37 +101,58 @@
     return jnp.where(place == rank, 1.0, 0.0)
 
 
-def exact_dot_t(values, table):
-    return lax.dot_general(
-        values, table, (((1,), (1,)), ((), ())), precision=HIGHEST, preferred_element_type=F32
+def dot_t(a, b):
+    return lax.dot_general(a, b, (((1,), (1,)), ((), ())), preferred_element_type=F32)
+
+
+def copy_in(pairs, sems):
+    copies = [pltpu.make_async_copy(src, dst, sems.at[k]) for k, (src, dst) in enumerate(pairs)]
+    for copy in copies:
+        copy.start()
+    return copies
+
+
+def planes_kernel(pos_any, table_any, orb_any, chg_any, out_ref, pos_ref, table, data, sems):
+    planes = out_ref.shape[0] // SLOTS
+    copies = copy_in(
+        [
+            (pos_any, pos_ref),
+            (orb_any.at[:, 0], data.at[0:2]),
+            (chg_any.at[:, 0], data.at[2:4]),
+            (table_any, table),
+        ],
+        sems,
     )
-
-
-def planes_kernel(table_ref, orb_ref, chg_ref, pos_ref, out_ref):
-    planes = table_ref.shape[0] // 2
-    depth = table_ref.shape[1]
-    both = jnp.concatenate(
-        [orb_ref[...].reshape(depth, LANES), chg_ref[...].reshape(depth, LANES)], axis=1
-    )
+    copies[0].wait()
     pos = pos_ref[...].astype(F32)
-    order = sort_table(pos)
-    pos = exact_dot_t(jnp.broadcast_to(pos, (SLOTS, LANES)), order)[0:1, :]
-    values = jnp.dot(table_ref[...], both, precision=HIGHEST, preferred_element_type=F32)
-    values = exact_dot_t(
-        jnp.concatenate([values[:, :LANES], values[:, LANES:]], axis=0), order
-    )
+    order = sort_table(pos).astype(BF16)
     row = jnp.floor((pos + 0.5) * (1.0 / GRID))
     col = pos - row * GRID
     row = row + 8.0 * (jnp.where(row >= THIRD, 1.0, 0.0) + jnp.where(row >= 2 * THIRD, 1.0, 0.0))
     col = col + 8.0 * (jnp.where(col >= THIRD, 1.0, 0.0) + jnp.where(col >= 2 * THIRD, 1.0, 0.0))
-    pieces = [values[k * planes : (k + 1) * planes] for k in range(4)] + [
-        jnp.broadcast_to(row, (planes, LANES)),
-        jnp.broadcast_to(col, (planes, LANES)),
-        jnp.zeros((planes, LANES), F32),
-        jnp.zeros((planes, LANES), F32),
-    ]
-    for slot, piece in enumerate(pieces):
-        out_ref[pl.ds(slot, planes, stride=SLOTS), :] = piece
+    place = jnp.concatenate([row, col, jnp.zeros((SLOTS - 2, LANES), F32)], axis=0)
+    high, low = halves(place)
+    place = dot_t(high, order) + dot_t(low, order)
+    for slot in range(4, SLOTS):
+        line = place[slot - 4 : slot - 3, :]
+        out_ref[pl.ds(slot, planes, stride=SLOTS), :] = jnp.broadcast_to(line, (planes, LANES))
+    for copy in copies[1:]:
+        copy.wait()
+    both = jnp.concatenate(
+        [
+            data[0:2].reshape(2 * GRID, LANES),
+            data[2:4].reshape(2 * GRID, LANES),
+        ],
+        axis=1,
+    )
+    high, low = halves(both)
+    values = dot3(table[0], table[1], high, low)
+    high, low = halves(jnp.concatenate([values[:, :LANES], values[:, LANES:]], axis=0))
+    values = dot_t(high, order) + dot_t(low, order)
+    for slot in range(4):
+        out_ref[pl.ds(slot, planes, stride=SLOTS), :] = values[
+            slot * planes : (slot + 1) * planes
+        ]
 
 
 def reorder_kernel(pot_ref, per_ref, order_ref, out_ref, lines, rows):
@@ -180,10 +199,47 @@
     return jnp.where(cols == vals[5:6, :], 1.0, 0.0).astype(BF16)
 
 
+def find_windows(group, win):
+    most = 0
+    for q in range(CHUNKS):
+        rows = group[q * SLOTS + 4 : q * SLOTS + 5, :]
+        low = jnp.min(rows).astype(jnp.int32)
+        high = jnp.max(rows).astype(jnp.int32)
+        start = jnp.bitwise_and(low, -16)
+        count = lax.shift_right_logical(high - start, 7) + 1
+        win[q] = start
+        win[CHUNKS + q] = count
+        most = jnp.maximum(most, count)
+    return most
+
+
+def over_windows(work, most, win):
+    @pl.when(most == 1)
+    def _():
+        def four(step, _):
+            for k in range(4):
+                work(4 * step + k, pl.multiple_of(win[4 * step + k], 16))
+            return 0
+
+        lax.fori_loop(0, CHUNKS // 4, four, 0)
+
+    @pl.when(most > 1)
+    def _():
+        def one(q, _):
+            def block(b, _):
+                work(q, pl.multiple_of(win[q] + b * WINDOW, 16))
+                return 0
+
+            lax.fori_loop(0, win[CHUNKS + q], block, 0)
+            return 0
+
+        lax.fori_loop(0, CHUNKS, one, 0)
+
+
 def forward_kernel(
     vals_ref, pot_ref, rh_ref, rl_ref, lh_ref, ll_ref,
-    keep_ref, send_ref, hh_ref, hl_ref, group_ref, win_ref,
-    field, xh, xl, zh, zl, dens,
+    keep_ref, send_ref, hh_ref, hl_ref, group_ref,
+    win_ref, field, xh, xl, zh, zl, dens,
 ):
     core = lax.axis_index("band") % 2
     field[...] = jnp.zeros_like(field)
@@ -194,17 +250,7 @@
         ]
         for q, block in enumerate(exchange_lanes(blocks)):
             group_ref[q * SLOTS : (q + 1) * SLOTS, half * LANES : (half + 1) * LANES] = block
-    most = 0
-    for q in range(CHUNKS):
-        rows = group_ref[q * SLOTS + 4 : q * SLOTS + 5, :]
-        low = jnp.min(rows).astype(jnp.int32)
-        high = jnp.max(rows).astype(jnp.int32)
-        start = jnp.bitwise_and(low, -16)
-        count = lax.shift_right_logical(high - start, 7) + 1
-        win_ref[q] = start
-        win_ref[CHUNKS + q] = count
-        most = jnp.maximum(most, count)
-    win_ref[2 * CHUNKS] = most
+    most = find_windows(group_ref, win_ref)
 
     def place(q, start):
         vals = group_ref[pl.ds(pl.multiple_of(q * SLOTS, SLOTS), SLOTS), :]
@@ -223,26 +269,7 @@
         for comp in range(4):
             field[comp, pl.ds(start, WINDOW), :] += placed[comp * WINDOW : (comp + 1) * WINDOW]
 
-    @pl.when(most == 1)
-    def _():
-        def four(step, _):
-            for k in range(4):
-                place(4 * step + k, pl.multiple_of(win_ref[4 * step + k], 16))
-            return 0
-
-        lax.fori_loop(0, CHUNKS // 4, four, 0)
-
-    @pl.when(most > 1)
-    def _():
-        def one(q, _):
-            def block(b, _):
-                place(q, pl.multiple_of(win_ref[q] + b * WINDOW, 16))
-                return 0
-
-            lax.fori_loop(0, win_ref[CHUNKS + q], block, 0)
-            return 0
-
-        lax.fori_loop(0, CHUNKS, one, 0)
+    over_windows(place, most, win_ref)
 
     step = 16
     for f in range(2):
@@ -294,15 +321,18 @@
             rows = slice(x2 * WIDE + k * LANES, x2 * WIDE + (k + 1) * LANES)
             hh_ref[rows, :] = high
             hl_ref[rows, :] = low
-    for m in range(4):
-        for x2 in range(3):
+        for m in range(4):
             own = pl.multiple_of(16 * (2 * m + core), 16)
             other = pl.multiple_of(16 * (2 * m + 1 - core), 16)
             keep_ref[m, 16 * x2 : 16 * (x2 + 1), :] = dens[x2, pl.ds(own, 16), :]
             send_ref[m, 16 * x2 : 16 * (x2 + 1), :] = dens[x2, pl.ds(other, 16), :]
 
 
-def back_kernel(hh_ref, hl_ref, lh_ref, ll_ref, rh_ref, rl_ref, out_ref, mid, ph, plow):
+def back_kernel(
+    group_ref, hh_ref, hl_ref, lh_ref, ll_ref, rh_ref, rl_ref, out_ref,
+    mid, ph, plow, grid, picked, win,
+):
+    grid[:, PAD:, :] = jnp.zeros((2, WINDOW, 2 * PAD), BF16)
     for x2 in range(3):
         at = slice(x2 * WIDE, (x2 + 1) * WIDE)
         mid[at, :] = dot3(lh_ref[at, :], ll_ref[at, :], hh_ref[at, :], hl_ref[at, :])
@@ -324,6 +354,7 @@
                     to = slice(y2 * WIDE + k * LANES, y2 * WIDE + (k + 1) * LANES)
                     ph[rows, to] = high
                     plow[rows, to] = low
+    most = find_windows(group_ref, win)
     for y2 in range(3):
         at = slice(y2 * WIDE, (y2 + 1) * WIDE)
         out = dot3(ph[:, at], plow[:, at], rh_ref[at, :], rl_ref[at, :])
@@ -340,57 +371,24 @@
         for q2, pair in enumerate(three_point(*parts, -1.0)):
             for k in range(2):
                 high, low = halves(pair[k])
-                out_ref[k, r : r + step, q2 * LANES : (q2 + 1) * LANES] = high
-                out_ref[k, r : r + step, PAD + q2 * LANES : PAD + (q2 + 1) * LANES] = low
-    out_ref[:, PAD:, :] = jnp.zeros((2, WINDOW, 2 * PAD), BF16)
-
-
-def pick_kernel(grid_ref, group_ref, win_ref, keep_ref, got_ref, out_ref, *rest):
-    block_refs, (picked, total) = rest[:4], rest[4:]
-    chip = lax.axis_index("band") // 2
-    total[...] = keep_ref[...] + got_ref[...]
-    for k in range(4):
-        block_refs[k][...] = total[jnp.bitwise_xor(chip, k)]
+                grid[k, r : r + step, q2 * LANES : (q2 + 1) * LANES] = high
+                grid[k, r : r + step, PAD + q2 * LANES : PAD + (q2 + 1) * LANES] = low
+    picked[...] = jnp.zeros_like(picked)
 
     def pick(q, start):
-        vals = group_ref[pl.ds(pl.multiple_of(q * SLOTS, SLOTS), SLOTS), :]
+        at = pl.ds(pl.multiple_of(q * SLOTS, SLOTS), SLOTS)
+        vals = group_ref[at, :]
         mask = window_rows(vals, start)
         cols = column_hot(vals)
-        lines = grid_ref[:, pl.ds(start, WINDOW), :].reshape(2 * WINDOW, 2 * PAD)
+        lines = grid[:, pl.ds(start, WINDOW), :].reshape(2 * WINDOW, 2 * PAD)
         chosen = dot(lines, jnp.concatenate([cols, cols], axis=0))
         real = jnp.sum(jnp.where(mask, chosen[:WINDOW], 0.0), axis=0, keepdims=True)
         imag = jnp.sum(jnp.where(mask, chosen[WINDOW:], 0.0), axis=0, keepdims=True)
-        return jnp.concatenate([real, imag, jnp.zeros((SLOTS - 2, WIDE), F32)], axis=0)
-
-    most = win_ref[2 * CHUNKS]
-
-    @pl.when(most == 1)
-    def _():
-        def four(step, _):
-            for k in range(4):
-                q = 4 * step + k
-                at = pl.ds(pl.multiple_of(q * SLOTS, SLOTS), SLOTS)
-                picked[at, :] = pick(q, pl.multiple_of(win_ref[q], 16))
-            return 0
-
-        lax.fori_loop(0, CHUNKS // 4, four, 0)
-
-    @pl.when(most > 1)
-    def _():
-        picked[...] = jnp.zeros_like(picked)
-
-        def one(q, _):
-            at = pl.ds(pl.multiple_of(q * SLOTS, SLOTS), SLOTS)
-
-            def block(b, _):
-                picked[at, :] += pick(q, pl.multiple_of(win_ref[q] + b * WINDOW, 16))
-                return 0
-
-            lax.fori_loop(0, win_ref[CHUNKS + q], block, 0)
-            return 0
-
-        lax.fori_loop(0, CHUNKS, one, 0)
-
+        picked[at, :] += jnp.concatenate(
+            [real, imag, jnp.zeros((SLOTS - 2, WIDE), F32)], axis=0
+        )
+
+    over_windows(pick, most, win)
     for half in range(2):
         blocks = [
             picked[q * SLOTS : (q + 1) * SLOTS, half * LANES : (half + 1) * LANES]
@@ -401,17 +399,21 @@
             out_ref[src * SLOTS : (src + 1) * SLOTS, :] = block
 
 
-def residual_kernel(table_ref, order_ref, back_ref, chg_ref, pos_ref, energy_ref, *rest):
-    parts = rest[:4]
-    out_ref, dens_ref = rest[4:]
+def pair_kernel(keep_ref, got_ref, *rest):
+    block_refs, total = rest[:4], rest[4]
+    chip = lax.axis_index("band") // 2
+    total[...] = keep_ref[...] + got_ref[...]
+    for k in range(4):
+        block_refs[k][...] = total[jnp.bitwise_xor(chip, k)]
+
+
+def residual_kernel(
+    pos_ref, table, order_ref, chg_ref, back_ref, energy_ref, *rest
+):
+    parts, (out_ref, dens_ref) = rest[:4], rest[4:]
     planes = back_ref.shape[0] // SLOTS
     pos = pos_ref[...].astype(F32)
-    order = sort_table(pos)
-    real = back_ref[pl.ds(0, planes, stride=SLOTS), :]
-    imag = back_ref[pl.ds(1, planes, stride=SLOTS), :]
-    both = jnp.concatenate([real, imag], axis=0)
-    both = jnp.dot(both, order, precision=HIGHEST, preferred_element_type=F32)
-    applied = jnp.dot(table_ref[...], both, precision=HIGHEST, preferred_element_type=F32)
+    order = sort_table(pos).astype(BF16)
     row = jnp.floor((pos + 0.5) * (1.0 / GRID))
     col = pos - row * GRID
     half = GRID // 2
@@ -421,12 +423,15 @@
     depth = jnp.where(depth < half, depth, depth - GRID)
     kinetic = (depth * depth + (row * row + col * col)) * (8.0 / (GRID * GRID))
     factor = kinetic - energy_ref[0]
-    out_ref[0, 0] = factor * chg_ref[0, 0] + applied[:GRID]
-    out_ref[1, 0] = factor * chg_ref[1, 0] + applied[GRID:]
+    real = back_ref[pl.ds(0, planes, stride=SLOTS), :]
+    imag = back_ref[pl.ds(1, planes, stride=SLOTS), :]
+    high, low = halves(jnp.concatenate([real, imag], axis=0))
+    both = dot(jnp.concatenate([high, low], axis=0), order).astype(BF16)
+    applied = dot(table[...], jnp.concatenate([both, both[: 2 * planes]], axis=0))
+    for k in range(2):
+        out_ref[k, 0] = factor * chg_ref[k, 0] + applied[k * GRID : (k + 1) * GRID]
     high, low = halves(parts[0][...] + parts[1][...] + parts[2][...] + parts[3][...])
-    turned = (((1,), (1,)), ((), ()))
-    total = lax.dot_general(high, order_ref[...], turned, preferred_element_type=F32)
-    total += lax.dot_general(low, order_ref[...], turned, preferred_element_type=F32)
+    total = dot_t(high, order_ref[...]) + dot_t(low, order_ref[...])
     for i in range(15):
         for x2 in range(3):
             dens_ref[3 * i + x2] = total[16 * x2 + i : 16 * x2 + i + 1, :GRID]
@@ -436,18 +441,22 @@
     return [pl.BlockSpec(memory_space=pltpu.VMEM)] * count
 
 
+def in_hbm(count):
+    return [pl.BlockSpec(memory_space=pltpu.HBM)] * count
+
+
 def in_smem():
     return pl.BlockSpec(memory_space=pltpu.SMEM)
 
 
-def call(kernel, name, outs, ins, out_specs, scratch=(), flops=0):
+def call(kernel, name, outs, ins, out_specs, scratch=(), flops=0, limit=32):
     return pl.pallas_call(
         kernel,
         out_shape=outs,
         in_specs=ins,
         out_specs=out_specs,
         scratch_shapes=list(scratch),
-        compiler_params=pltpu.CompilerParams(vmem_limit_bytes=VMEM_LIMIT),
+        compiler_params=pltpu.CompilerParams(vmem_limit_bytes=limit * 1024 * 1024),
         cost_estimate=pl.CostEstimate(flops=flops, bytes_accessed=3_000_000, transcendentals=0),
         name=name,
     )
@@ -455,6 +464,10 @@
 
 def shape(*dims, dtype=F32):
     return jax.ShapeDtypeStruct(dims, dtype)
+
+
+def sems(count):
+    return pltpu.SemaphoreType.DMA((count,))
 
 
 def on_device(orbitals, response, potential, perturbation, energies, stick_pos):
@@ -462,25 +475,47 @@
     bands = lax.axis_size("band")
     cos, sin = trig(np.arange(planes), np.arange(GRID))
     to_planes = np.block([[cos, -sin], [sin, cos]]) / math.sqrt(GRID)
+    to_planes = np.stack(split_table(to_planes))
     from_planes = np.block([[cos.T, sin.T], [-sin.T, cos.T]]) / math.sqrt(planes)
+    high, low = split_table(from_planes)
+    from_planes = np.concatenate([high, high, low], axis=1)
     right, left, left_back, right_back = transform_tables()
     order = column_order()
     pos = stick_pos.reshape(1, LANES)
+    square = pltpu.VMEM((2 * PAD, 2 * PAD), BF16)
+    grouped = pltpu.VMEM((CHUNKS * SLOTS, WIDE), F32)
+    windows = pltpu.SMEM((2 * CHUNKS,), jnp.int32)
 
     packed = call(
-        planes_kernel, "to_planes", shape(planes * SLOTS, LANES), in_vmem(4), in_vmem(1)[0],
+        planes_kernel,
+        "to_planes",
+        shape(planes * SLOTS, LANES),
+        in_hbm(4),
+        in_vmem(1)[0],
+        [
+            pltpu.VMEM((1, LANES), jnp.int32),
+            pltpu.VMEM(to_planes.shape, BF16),
+            pltpu.VMEM((4, GRID, LANES), F32),
+            sems(4),
+        ],
         flops=500_000_000,
-    )(to_planes.astype(np.float32), orbitals, response, pos)
+        limit=60,
+    )(pos, to_planes, orbitals, response)
     arrived = lax.all_to_all(
         packed.reshape(planes, SLOTS, LANES), "pw", split_axis=0, concat_axis=0, tiled=True
     ).reshape(planes * SLOTS, LANES)
     pots = call(
-        reorder_kernel, "reorder", shape(2, PAD, PAD), in_vmem(3), in_vmem(1)[0],
+        reorder_kernel,
+        "reorder",
+        shape(2, PAD, PAD),
+        in_vmem(3),
+        in_vmem(1)[0],
         [pltpu.VMEM((3 * GRID, LANES), F32), pltpu.VMEM((PAD, PAD), F32)],
         flops=1_500_000_000,
+        limit=60,
     )(potential, perturbation, order)
 
-    keep, send, h_high, h_low, group, windows = call(
+    keep, send, h_high, h_low, group = call(
         forward_kernel,
         "place_and_transform",
         [
@@ -489,46 +524,43 @@
             shape(2 * PAD, PAD, dtype=BF16),
             shape(2 * PAD, PAD, dtype=BF16),
             shape(CHUNKS * SLOTS, WIDE),
-            shape(2 * CHUNKS + 1, dtype=jnp.int32),
         ],
         in_vmem(6),
-        in_vmem(5) + [in_smem()],
-        [
-            pltpu.VMEM((4, TALL, PAD), F32),
-            pltpu.VMEM((2 * PAD, 2 * PAD), BF16),
-            pltpu.VMEM((2 * PAD, 2 * PAD), BF16),
-            pltpu.VMEM((2 * PAD, 2 * PAD), BF16),
-            pltpu.VMEM((2 * PAD, 2 * PAD), BF16),
-            pltpu.VMEM((3, LANES, PAD), F32),
-        ],
+        in_vmem(5),
+        [windows, pltpu.VMEM((4, TALL, PAD), F32)]
+        + [square] * 4
+        + [pltpu.VMEM((3, LANES, PAD), F32)],
         flops=10_000_000_000,
     )(arrived, pots, *right, *left)
     got = lax.ppermute(send, "band", [(i, i ^ 1) for i in range(bands)])
-    grid = call(
+    picked = call(
         back_kernel,
-        "back",
-        shape(2, TALL, 2 * PAD, dtype=BF16),
-        in_vmem(6),
+        "back_and_pick",
+        shape(planes * SLOTS, LANES),
+        in_vmem(7),
         in_vmem(1)[0],
         [
             pltpu.VMEM((2 * PAD, PAD), F32),
             pltpu.VMEM((PAD, 2 * PAD), BF16),
             pltpu.VMEM((PAD, 2 * PAD), BF16),
+            pltpu.VMEM((2, TALL, 2 * PAD), BF16),
+            grouped,
+            windows,
         ],
-        flops=3_000_000_000,
-    )(h_high, h_low, *left_back, *right_back)
-    picked, *blocks = call(
-        pick_kernel,
-        "pick",
-        [shape(planes * SLOTS, LANES)] + [shape(48, PAD)] * 4,
-        in_vmem(2) + [in_smem()] + in_vmem(2),
-        in_vmem(5),
-        [pltpu.VMEM((CHUNKS * SLOTS, WIDE), F32), pltpu.VMEM((4, 48, PAD), F32)],
-        flops=5_000_000_000,
-    )(grid, group, windows, keep, got)
+        flops=6_000_000_000,
+    )(group, h_high, h_low, *left_back, *right_back)
     returned = lax.all_to_all(
         picked.reshape(planes, SLOTS, LANES), "pw", split_axis=0, concat_axis=0, tiled=True
     ).reshape(planes * SLOTS, LANES)
+    blocks = call(
+        pair_kernel,
+        "pair_sum",
+        [shape(48, PAD)] * 4,
+        in_vmem(2),
+        in_vmem(4),
+        [pltpu.VMEM((4, 48, PAD), F32)],
+        flops=300_000,
+    )(keep, got)
     parts = [blocks[0]] + [
         lax.ppermute(blocks[k], "band", [(i, i ^ (2 * k)) for i in range(bands)])
         for k in range(1, 4)
@@ -541,7 +573,7 @@
         in_vmem(5) + [in_smem()] + in_vmem(4),
         in_vmem(2),
         flops=500_000_000,
-    )(from_planes.astype(np.float32), order, returned, response, pos, energies, *parts)
+    )(pos, from_planes, order, response, returned, energies, *parts)
     return (residual, density.reshape(1, GRID // bands, GRID))
 
 

time: 68.2 us -> 58 us (0.85)
  Pallas kernels: 31.3 us -> 21.9 us
  local copies, waits for them, and re-layouts: 2.03 us -> 1.33 us
    ppermute x3, waiting for transfers between devices: 4.94 us -> 0.01 us  [on_device(): lax.ppermute(blocks[k], 'band', [(i, i ^ 2 * k) for i in range(bands)])]
    all_to_all x1, waiting for transfers between devices: 0.22 us -> 5.12 us  [on_device(): lax.all_to_all(picked.reshape(planes, SLOTS, LANES), 'pw', split_axis=0,...]
    pallas_call x3, Pallas kernels: 12.5 us -> 7.67 us  [the longest x1 5.23 us: on_device(): call(back_kernel, 'back_and_pick', shape(planes * SLOTS, LANES), in_vmem(...]
    pallas_call x1, Pallas kernels: 12.5 us -> 9.48 us  [on_device(): call(forward_kernel, 'place_and_transform', [shape(4, 48, PAD), shape(4,...]
    pallas_call x1, Pallas kernels: 3.02 us -> 1.35 us  [on_device(): call(residual_kernel, 'from_planes', [shape(2, 1, GRID, LANES), shape(GRI...]
    unnamed x12 -> x26, local copies, waits for them, and re-layouts: 2.03 us -> 1.33 us
  transfers between devices with their start and end apart: 6 -> 6, of which waited for: 4 -> 2; matrix products, arithmetic and copies ran while one was open for 0% -> 0% of each run, Pallas kernels for 12% -> 15%
where the time goes in v1:
time: 58 us; the launch traced here: 57.6 us
  Pallas kernels  21.9 us (38%)
  starting transfers between devices  21.9 us (38%)
  waiting for transfers between devices  11 us (19%)
  between operations  1.46 us (3%)
  local copies, waits for them, and re-layouts  1.33 us (2%)
    all_to_all x1, starting transfers between devices, on_device(): lax.all_to_all(packed.reshape(planes, SLOTS, LANES), 'pw', split_axis=0,...  11.9 us
    pallas_call x1, Pallas kernels, on_device(): call(forward_kernel, 'place_and_transform', [shape(4, 48, PAD), shape(4,...  9.48 us
    all_to_all x1, waiting for transfers between devices, on_device(): lax.all_to_all(packed.reshape(planes, SLOTS, LANES), 'pw', split_axis=0,...  5.86 us
    pallas_call x1, Pallas kernels, on_device(): call(back_kernel, 'back_and_pick', shape(planes * SLOTS, LANES), in_vmem(...  5.23 us
    all_to_all x1, waiting for transfers between devices, on_device(): lax.all_to_all(picked.reshape(planes, SLOTS, LANES), 'pw', split_axis=0,...  5.12 us
    ppermute x3, starting transfers between devices, on_device(): lax.ppermute(blocks[k], 'band', [(i, i ^ 2 * k) for i in range(bands)])  4.01 us
    all_to_all x1, starting transfers between devices, on_device(): lax.all_to_all(picked.reshape(planes, SLOTS, LANES), 'pw', split_axis=0,...  3.86 us
    pallas_call x1, Pallas kernels, on_device(): call(reorder_kernel, 'reorder', shape(2, PAD, PAD), in_vmem(3), in_vmem(1...  3.43 us
  transfers between devices with their start and end apart: 6, of which 2 were waited for; matrix products, arithmetic and copies ran while one was open for 0% of the time, Pallas kernels for 15%

profile of v1, /device:TPU:1, one launch (start us, length us, event | category | flops | bytes accessed | tf_op | source)
XLA Modules:
  0.0 57.6 jit_solution(15051438551338466295)
XLA Ops:
  0.6 2.4 %to_planes.1 = f32[256,128]{1,0:T(8,128)} custom-call(s32[1,128]{1,0:T(1,128)} %bitcast.8, bf16[2,64,720]{2,1,0:T(8,128)(2,1)} %constant.22.clone.table_any, f32[2,1,360,128]{3,2,1,0:T(8,128)} %orb_any.1, f32[2,1,360,128]{3,2,1,0:T(8,128)} %chg_ref.1), custom_call_target="tpu_custom_call" | custom-call | flops 500000000 | bytes 3000000 | tf_op jit(solution)/shard_map/to_planes/pallas_call | solution.py:489
  3.0 11.9 %all-to-all-start = ((f32[32,8,128]{2,1,0:T(8,128)}), f32[32,8,128]{2,1,0:T(8,128)S(1)}, u32[]{:S(2)}, u32[]{:S(2)}) async-start(f32[32,8,128]{2,1,0:T(8,128)} %bitcast.10), calls=%async_computation | async-start | bytes 262144 | tf_op jit(solution)/shard_map/all_to_all | solution.py:504
  14.9 0.0 copy-start.6
  14.9 0.0 copy-start.7
  14.9 0.0 copy-start.8
  14.9 0.0 copy-start.9
  15.0 3.4 %reorder.1.pot_ref = f32[2,384,384]{2,1,0:T(8,128)} custom-call(f32[1,360,360]{2,1,0:T(8,128)} %pot_ref.1, f32[1,360,360]{2,1,0:T(8,128)} %per_ref.1, bf16[384,384]{1,0:T(8,128)(2,1)} %constant.23.clone.order_ref), custom_call_target="tpu_custom_call" | custom-call | flops 1500000000 | bytes 3000000 | tf_op jit(solution)/shard_map/reorder/pallas_call | solution.py:507
  18.4 5.9 %all-to-all-done = f32[32,8,128]{2,1,0:T(8,128)S(1)} async-done(((f32[32,8,128]{2,1,0:T(8,128)}), f32[32,8,128]{2,1,0:T(8,128)S(1)}, u32[]{:S(2)}, u32[]{:S(2)}) %all-to-all-start) | async-done | bytes 131104 | tf_op jit(solution)/shard_map/all_to_all | solution.py:504
  24.3 1.3 %copy-done.12 = f32[2,384,384]{2,1,0:T(8,128)S(1)} copy-done((f32[2,384,384]{2,1,0:T(8,128)S(1)}, f32[2,384,384]{2,1,0:T(8,128)}, u32[]{:S(2)}) %copy-start.12) | copy-done | bytes 1179672
  25.6 9.5 %place_and_transform.1 = (f32[4,48,384]{2,1,0:T(8,128)S(1)}, f32[4,48,384]{2,1,0:T(8,128)S(1)}, bf16[768,384]{1,0:T(8,128)(2,1)S(1)}, bf16[768,384]{1,0:T(8,128)(2,1)S(1)}, f32[128,256]{1,0:T(8,128)S(1)}) custom-call(f32[256,128]{1,0:T(8,128)S(1)} %bitcast.7, f32[2,384,384]{2,1,0:T(8,128)S(1)} %copy-done.12, bf16[768,256]{1,0:T(8,128)(2,1)S(1)} %copy-done.6, ...), custom_call_target="tpu_custom_call" | custom-call | flops 10000000000 | bytes 3000000 | tf_op jit(solution)/shard_map/place_and_transform/pallas_call | solution.py:518
  35.0 2.1 %collective-permute-start = (f32[4,48,384]{2,1,0:T(8,128)S(1)}, f32[4,48,384]{2,1,0:T(8,128)S(1)}, u32[]{:S(2)}, u32[]{:S(2)}) collective-permute-start(f32[4,48,384]{2,1,0:T(8,128)S(1)} %get-tuple-element.17), channel_id=1, source_target_pairs={{0,32},{32,0},{64,96},{96,64},{128,160},{160,128},{192,224},{224,1... | collective-permute-start | bytes 884744 | tf_op jit(solution)/shard_map/ppermute | solution.py:535
  37.2 0.0 copy-start
  37.2 0.0 copy-start.1
  37.2 0.0 copy-start.10
  37.2 0.0 copy-start.11
  37.2 5.2 %back_and_pick.1 = f32[256,128]{1,0:T(8,128)} custom-call(f32[128,256]{1,0:T(8,128)S(1)} %get-tuple-element.13.group_ref, bf16[768,384]{1,0:T(8,128)(2,1)S(1)} %get-tuple-element.14.hh_ref, bf16[768,384]{1,0:T(8,128)(2,1)S(1)} %get-tuple-element.15.hl_ref, bf16[768,256]{1,0:T(8,128)(2,1)S(1)} %copy-done.2, bf16[768,256]{1,0:T(8,128)(2,1)S(1)} %copy-done.3, ...), custom_call_target="tpu_custom_call" | custom-call | flops 6000000000 | bytes 3000000 | tf_op jit(solution)/shard_map/back_and_pick/pallas_call | solution.py:536
  42.5 3.9 %all-to-all-start.1 = ((f32[32,8,128]{2,1,0:T(8,128)}), f32[32,8,128]{2,1,0:T(8,128)S(1)}, u32[]{:S(2)}, u32[]{:S(2)}) async-start(f32[32,8,128]{2,1,0:T(8,128)} %bitcast.3), calls=%async_computation.1 | async-start | bytes 262144 | tf_op jit(solution)/shard_map/all_to_all | solution.py:552
  46.3 0.0 collective-permute-done.got_ref
  46.4 0.1 pair_sum.1
  46.4 1.4 %collective-permute-start.1 = (f32[48,384]{1,0:T(8,128)S(1)}, f32[48,384]{1,0:T(8,128)S(1)}, u32[]{:S(2)}, u32[]{:S(2)}) collective-permute-start(f32[48,384]{1,0:T(8,128)S(1)} %get-tuple-element.19), channel_id=1, source_target_pairs={{0,64},{32,96},{64,0},{96,32},{128,192},{160,224},{192,128},{224,1... | collective-permute-start | bytes 221192 | tf_op jit(solution)/shard_map/ppermute | solution.py:565
  47.8 2.6 %collective-permute-start.2 = (f32[48,384]{1,0:T(8,128)S(1)}, f32[48,384]{1,0:T(8,128)S(1)}, u32[]{:S(2)}, u32[]{:S(2)}) collective-permute-start(f32[48,384]{1,0:T(8,128)S(1)} %get-tuple-element.20), channel_id=1, source_target_pairs={{0,128},{32,160},{64,192},{96,224},{128,0},{160,32},{192,64},{224,... | collective-permute-start | bytes 221192 | tf_op jit(solution)/shard_map/ppermute | solution.py:565
  50.4 0.0 collective-permute-start.3
  51.1 5.1 %all-to-all-done.1 = f32[32,8,128]{2,1,0:T(8,128)S(1)} async-done(((f32[32,8,128]{2,1,0:T(8,128)}), f32[32,8,128]{2,1,0:T(8,128)S(1)}, u32[]{:S(2)}, u32[]{:S(2)}) %all-to-all-start.1) | async-done | bytes 131104 | tf_op jit(solution)/shard_map/all_to_all | solution.py:552
  56.2 1.3 %from_planes.1 = (f32[2,1,360,128]{3,2,1,0:T(8,128)}, f32[45,1,360]{2,1,0:T(1,128)}) custom-call(s32[1,128]{1,0:T(1,128)S(1)} %bitcast.9, bf16[720,192]{1,0:T(8,128)(2,1)S(1)} %copy-done.10, bf16[384,384]{1,0:T(8,128)(2,1)S(1)} %copy-done.11, f32[2,1,360,128]{3,2,1,0:T(8,128)S(1)} %copy-done, f32[256,128]{1,0:T(8,128)S(1)} %bitcast.6, ...), custom_call_target="tpu_custom_call" | custom-call | flops 500000000 | bytes 3000000 | tf_op jit(solution)/shard_map/from_planes/pallas_call | solution.py:569
  (20 shorter events, 0.0 us)
Async XLA Ops:
  3.0 21.2 %all-to-all-start = ((f32[32,8,128]{2,1,0:T(8,128)}), f32[32,8,128]{2,1,0:T(8,128)S(1)}, u32[]{:S(2)}, u32[]{:S(2)}) async-start(f32[32,8,128]{2,1,0:T(8,128)} %bitcast.10), calls=%async_computation | async-start | bytes 262144 | tf_op jit(solution)/shard_map/all_to_all | solution.py:504
  14.9 9.3 %copy-start.6 = (bf16[768,256]{1,0:T(8,128)(2,1)S(1)}, bf16[768,256]{1,0:T(8,128)(2,1)}, u32[]{:S(2)}) copy-start(bf16[768,256]{1,0:T(8,128)(2,1)} %constant.24.clone.rh_ref) | copy-start | bytes 1179652
  14.9 9.3 %copy-start.7 = (bf16[768,256]{1,0:T(8,128)(2,1)S(1)}, bf16[768,256]{1,0:T(8,128)(2,1)}, u32[]{:S(2)}) copy-start(bf16[768,256]{1,0:T(8,128)(2,1)} %constant.25.clone.rl_ref) | copy-start | bytes 1179652
  14.9 9.3 %copy-start.8 = (bf16[768,256]{1,0:T(8,128)(2,1)S(1)}, bf16[768,256]{1,0:T(8,128)(2,1)}, u32[]{:S(2)}) copy-start(bf16[768,256]{1,0:T(8,128)(2,1)} %constant.26.clone.lh_ref) | copy-start | bytes 1179652
  14.9 9.3 %copy-start.9 = (bf16[768,256]{1,0:T(8,128)(2,1)S(1)}, bf16[768,256]{1,0:T(8,128)(2,1)}, u32[]{:S(2)}) copy-start(bf16[768,256]{1,0:T(8,128)(2,1)} %constant.27.clone.ll_ref) | copy-start | bytes 1179652
  24.3 1.3 %copy-start.12 = (f32[2,384,384]{2,1,0:T(8,128)S(1)}, f32[2,384,384]{2,1,0:T(8,128)}, u32[]{:S(2)}) copy-start(f32[2,384,384]{2,1,0:T(8,128)} %reorder.1.pot_ref) | copy-start | bytes 3538948
  25.6 11.6 %copy-start.2 = (bf16[768,256]{1,0:T(8,128)(2,1)S(1)}, bf16[768,256]{1,0:T(8,128)(2,1)}, u32[]{:S(2)}) copy-start(bf16[768,256]{1,0:T(8,128)(2,1)} %constant.28.clone.lh_ref) | copy-start | bytes 1179652
  25.6 11.6 %copy-start.3 = (bf16[768,256]{1,0:T(8,128)(2,1)S(1)}, bf16[768,256]{1,0:T(8,128)(2,1)}, u32[]{:S(2)}) copy-start(bf16[768,256]{1,0:T(8,128)(2,1)} %constant.29.clone.ll_ref) | copy-start | bytes 1179652
  25.6 11.6 %copy-start.4 = (bf16[768,256]{1,0:T(8,128)(2,1)S(1)}, bf16[768,256]{1,0:T(8,128)(2,1)}, u32[]{:S(2)}) copy-start(bf16[768,256]{1,0:T(8,128)(2,1)} %constant.30.clone.rh_ref) | copy-start | bytes 1179652
  25.6 11.6 %copy-start.5 = (bf16[768,256]{1,0:T(8,128)(2,1)S(1)}, bf16[768,256]{1,0:T(8,128)(2,1)}, u32[]{:S(2)}) copy-start(bf16[768,256]{1,0:T(8,128)(2,1)} %constant.31.clone.rl_ref) | copy-start | bytes 1179652
  35.0 11.3 %collective-permute-start = (f32[4,48,384]{2,1,0:T(8,128)S(1)}, f32[4,48,384]{2,1,0:T(8,128)S(1)}, u32[]{:S(2)}, u32[]{:S(2)}) collective-permute-start(f32[4,48,384]{2,1,0:T(8,128)S(1)} %get-tuple-element.17), channel_id=1, source_target_pairs={{0,32},{32,0},{64,96},{96,64},{128,160},{160,128},{192,224},{224,1... | collective-permute-start | bytes 884744 | tf_op jit(solution)/shard_map/ppermute | solution.py:535
  37.2 19.0 %copy-start = (f32[2,1,360,128]{3,2,1,0:T(8,128)S(1)}, f32[2,1,360,128]{3,2,1,0:T(8,128)}, u32[]{:S(2)}) copy-start(f32[2,1,360,128]{3,2,1,0:T(8,128)} %chg_ref.1) | copy-start | bytes 1105924
  37.2 19.0 %copy-start.1 = (s32[128]{0:T(128)S(1)}, s32[128]{0:T(128)}, u32[]{:S(2)}) copy-start(s32[128]{0:T(128)} %param.22) | copy-start | bytes 1540
  37.2 19.0 %copy-start.10 = (bf16[720,192]{1,0:T(8,128)(2,1)S(1)}, bf16[720,192]{1,0:T(8,128)(2,1)}, u32[]{:S(2)}) copy-start(bf16[720,192]{1,0:T(8,128)(2,1)} %constant.32.clone.table) | copy-start | bytes 829444
  37.2 19.0 %copy-start.11 = (bf16[384,384]{1,0:T(8,128)(2,1)S(1)}, bf16[384,384]{1,0:T(8,128)(2,1)}, u32[]{:S(2)}) copy-start(bf16[384,384]{1,0:T(8,128)(2,1)} %constant.23.clone.order_ref) | copy-start | bytes 884740
  42.5 13.7 %all-to-all-start.1 = ((f32[32,8,128]{2,1,0:T(8,128)}), f32[32,8,128]{2,1,0:T(8,128)S(1)}, u32[]{:S(2)}, u32[]{:S(2)}) async-start(f32[32,8,128]{2,1,0:T(8,128)} %bitcast.3), calls=%async_computation.1 | async-start | bytes 262144 | tf_op jit(solution)/shard_map/all_to_all | solution.py:552
  46.4 9.8 %collective-permute-start.1 = (f32[48,384]{1,0:T(8,128)S(1)}, f32[48,384]{1,0:T(8,128)S(1)}, u32[]{:S(2)}, u32[]{:S(2)}) collective-permute-start(f32[48,384]{1,0:T(8,128)S(1)} %get-tuple-element.19), channel_id=1, source_target_pairs={{0,64},{32,96},{64,0},{96,32},{128,192},{160,224},{192,128},{224,1... | collective-permute-start | bytes 221192 | tf_op jit(solution)/shard_map/ppermute | solution.py:565
  47.8 8.4 %collective-permute-start.2 = (f32[48,384]{1,0:T(8,128)S(1)}, f32[48,384]{1,0:T(8,128)S(1)}, u32[]{:S(2)}, u32[]{:S(2)}) collective-permute-start(f32[48,384]{1,0:T(8,128)S(1)} %get-tuple-element.20), channel_id=1, source_target_pairs={{0,128},{32,160},{64,192},{96,224},{128,0},{160,32},{192,64},{224,... | collective-permute-start | bytes 221192 | tf_op jit(solution)/shard_map/ppermute | solution.py:565
  50.4 5.8 %collective-permute-start.3 = (f32[48,384]{1,0:T(8,128)S(1)}, f32[48,384]{1,0:T(8,128)S(1)}, u32[]{:S(2)}, u32[]{:S(2)}) collective-permute-start(f32[48,384]{1,0:T(8,128)S(1)} %get-tuple-element.21), channel_id=1, source_target_pairs={{0,192},{32,224},{64,128},{96,160},{128,64},{160,96},{192,0},{224,... | collective-permute-start | bytes 221192 | tf_op jit(solution)/shard_map/ppermute | solution.py:565

commit v2 on v1

--- a/solution.py
+++ b/solution.py
@@ -18,6 +18,7 @@
 SLOTS = 8
 LANES = 128
 WINDOW = 128
+FIRST = (64, 96, 112) + (128,) * 10 + (112, 96, 80)
 TALL = PAD + WINDOW
 GROUP = 8
 CHUNKS = LANES // GROUP
@@ -155,7 +156,8 @@
         ]
 
 
-def reorder_kernel(pot_ref, per_ref, order_ref, out_ref, lines, rows):
+def reorder_kernel(pot_ref, per_ref, order_ref, out_ref, done_ref, lines, rows):
+    done_ref[0] = 0
     rows[...] = jnp.zeros_like(rows)
     lines[2 * GRID :, :] = jnp.zeros((GRID, LANES), F32)
     for field, ref in enumerate((pot_ref, per_ref)):
@@ -189,8 +191,8 @@
     return blocks
 
 
-def window_rows(vals, start):
-    rows = lax.broadcasted_iota(jnp.int32, (WINDOW, WIDE), 0) + start
+def window_rows(vals, start, count):
+    rows = lax.broadcasted_iota(jnp.int32, (count, WIDE), 0) + start
     return rows.astype(F32) == vals[4:5, :]
 
 
@@ -206,39 +208,34 @@
         low = jnp.min(rows).astype(jnp.int32)
         high = jnp.max(rows).astype(jnp.int32)
         start = jnp.bitwise_and(low, -16)
-        count = lax.shift_right_logical(high - start, 7) + 1
+        more = lax.shift_right_logical(high - start + (WINDOW - FIRST[q]), 7)
         win[q] = start
-        win[CHUNKS + q] = count
-        most = jnp.maximum(most, count)
+        win[CHUNKS + q] = start + FIRST[q]
+        win[2 * CHUNKS + q] = more
+        most = jnp.maximum(most, more)
     return most
 
 
 def over_windows(work, most, win):
-    @pl.when(most == 1)
-    def _():
-        def four(step, _):
-            for k in range(4):
-                work(4 * step + k, pl.multiple_of(win[4 * step + k], 16))
-            return 0
-
-        lax.fori_loop(0, CHUNKS // 4, four, 0)
-
-    @pl.when(most > 1)
+    for q in range(CHUNKS):
+        work(q, pl.multiple_of(win[q], 16), FIRST[q], True)
+
+    @pl.when(most > 0)
     def _():
         def one(q, _):
             def block(b, _):
-                work(q, pl.multiple_of(win[q] + b * WINDOW, 16))
+                work(q, pl.multiple_of(win[CHUNKS + q] + b * WINDOW, 16), WINDOW, False)
                 return 0
 
-            lax.fori_loop(0, win[CHUNKS + q], block, 0)
+            lax.fori_loop(0, win[2 * CHUNKS + q], block, 0)
             return 0
 
         lax.fori_loop(0, CHUNKS, one, 0)
 
 
 def forward_kernel(
-    vals_ref, pot_ref, rh_ref, rl_ref, lh_ref, ll_ref,
-    keep_ref, send_ref, hh_ref, hl_ref, group_ref,
+    done_ref, vals_ref, rh_ref, rl_ref, lh_ref, ll_ref,
+    keep_ref, send_ref, real_ref, group_ref,
     win_ref, field, xh, xl, zh, zl, dens,
 ):
     core = lax.axis_index("band") % 2
@@ -252,9 +249,9 @@
             group_ref[q * SLOTS : (q + 1) * SLOTS, half * LANES : (half + 1) * LANES] = block
     most = find_windows(group_ref, win_ref)
 
-    def place(q, start):
-        vals = group_ref[pl.ds(pl.multiple_of(q * SLOTS, SLOTS), SLOTS), :]
-        hot = jnp.where(window_rows(vals, start), 1.0, 0.0).astype(BF16)
+    def place(q, start, count, first):
+        vals = group_ref[pl.ds(q * SLOTS if first else pl.multiple_of(q * SLOTS, SLOTS), SLOTS), :]
+        hot = jnp.where(window_rows(vals, start, count), 1.0, 0.0).astype(BF16)
         cols = column_hot(vals)
         scaled = []
         for comp in range(4):
@@ -267,7 +264,7 @@
             preferred_element_type=F32,
         )
         for comp in range(4):
-            field[comp, pl.ds(start, WINDOW), :] += placed[comp * WINDOW : (comp + 1) * WINDOW]
+            field[comp, pl.ds(start, count), :] += placed[comp * count : (comp + 1) * count]
 
     over_windows(place, most, win_ref)
 
@@ -311,16 +308,8 @@
     for x2 in range(3):
         at = slice(x2 * WIDE, (x2 + 1) * WIDE)
         out = dot3(lh_ref[at, :], ll_ref[at, :], zh[at, :], zl[at, :])
-        orb_r, chg_r = out[:LANES, :PAD], out[:LANES, PAD:]
-        orb_i, chg_i = out[LANES:, :PAD], out[LANES:, PAD:]
-        dens[x2] = 2.0 * (orb_r * chg_r + orb_i * chg_i)
-        pot = pot_ref[0, x2 * LANES : (x2 + 1) * LANES, :]
-        per = pot_ref[1, x2 * LANES : (x2 + 1) * LANES, :]
-        for k, (chg, orb) in enumerate(((chg_r, orb_r), (chg_i, orb_i))):
-            high, low = halves(pot * chg + per * orb)
-            rows = slice(x2 * WIDE + k * LANES, x2 * WIDE + (k + 1) * LANES)
-            hh_ref[rows, :] = high
-            hl_ref[rows, :] = low
+        real_ref[at, :] = out
+        dens[x2] = 2.0 * (out[:LANES, :PAD] * out[:LANES, PAD:] + out[LANES:, :PAD] * out[LANES:, PAD:])
         for m in range(4):
             own = pl.multiple_of(16 * (2 * m + core), 16)
             other = pl.multiple_of(16 * (2 * m + 1 - core), 16)
@@ -329,13 +318,18 @@
 
 
 def back_kernel(
-    group_ref, hh_ref, hl_ref, lh_ref, ll_ref, rh_ref, rl_ref, out_ref,
+    group_ref, real_ref, pot_ref, lh_ref, ll_ref, rh_ref, rl_ref, out_ref, done_ref,
     mid, ph, plow, grid, picked, win,
 ):
+    done_ref[0] = 0
     grid[:, PAD:, :] = jnp.zeros((2, WINDOW, 2 * PAD), BF16)
     for x2 in range(3):
         at = slice(x2 * WIDE, (x2 + 1) * WIDE)
-        mid[at, :] = dot3(lh_ref[at, :], ll_ref[at, :], hh_ref[at, :], hl_ref[at, :])
+        rows = slice(x2 * LANES, (x2 + 1) * LANES)
+        pot = jnp.concatenate([pot_ref[0, rows, :]] * 2, axis=0)
+        per = jnp.concatenate([pot_ref[1, rows, :]] * 2, axis=0)
+        high, low = halves(pot * real_ref[at, PAD:] + per * real_ref[at, :PAD])
+        mid[at, :] = dot3(lh_ref[at, :], ll_ref[at, :], high, low)
     step = 16
     for r in range(0, LANES, step):
         for y2 in range(3):
@@ -373,20 +367,18 @@
                 high, low = halves(pair[k])
                 grid[k, r : r + step, q2 * LANES : (q2 + 1) * LANES] = high
                 grid[k, r : r + step, PAD + q2 * LANES : PAD + (q2 + 1) * LANES] = low
-    picked[...] = jnp.zeros_like(picked)
-
-    def pick(q, start):
-        at = pl.ds(pl.multiple_of(q * SLOTS, SLOTS), SLOTS)
+
+    def pick(q, start, count, first):
+        at = pl.ds(q * SLOTS if first else pl.multiple_of(q * SLOTS, SLOTS), SLOTS)
         vals = group_ref[at, :]
-        mask = window_rows(vals, start)
+        mask = window_rows(vals, start, count)
         cols = column_hot(vals)
-        lines = grid[:, pl.ds(start, WINDOW), :].reshape(2 * WINDOW, 2 * PAD)
+        lines = grid[:, pl.ds(start, count), :].reshape(2 * count, 2 * PAD)
         chosen = dot(lines, jnp.concatenate([cols, cols], axis=0))
-        real = jnp.sum(jnp.where(mask, chosen[:WINDOW], 0.0), axis=0, keepdims=True)
-        imag = jnp.sum(jnp.where(mask, chosen[WINDOW:], 0.0), axis=0, keepdims=True)
-        picked[at, :] += jnp.concatenate(
-            [real, imag, jnp.zeros((SLOTS - 2, WIDE), F32)], axis=0
-        )
+        real = jnp.sum(jnp.where(mask, chosen[:count], 0.0), axis=0, keepdims=True)
+        imag = jnp.sum(jnp.where(mask, chosen[count:], 0.0), axis=0, keepdims=True)
+        found = jnp.concatenate([real, imag, jnp.zeros((SLOTS - 2, WIDE), F32)], axis=0)
+        picked[at, :] = found if first else picked[at, :] + found
 
     over_windows(pick, most, win)
     for half in range(2):
@@ -396,10 +388,10 @@
         ]
         for j, block in enumerate(exchange_lanes(blocks)):
             src = half * CHUNKS + j
-            out_ref[src * SLOTS : (src + 1) * SLOTS, :] = block
-
-
-def pair_kernel(keep_ref, got_ref, *rest):
+            out_ref[2 * src : 2 * src + 2, :] = block[0:2, :]
+
+
+def pair_kernel(done_ref, keep_ref, got_ref, *rest):
     block_refs, total = rest[:4], rest[4]
     chip = lax.axis_index("band") // 2
     total[...] = keep_ref[...] + got_ref[...]
@@ -411,7 +403,7 @@
     pos_ref, table, order_ref, chg_ref, back_ref, energy_ref, *rest
 ):
     parts, (out_ref, dens_ref) = rest[:4], rest[4:]
-    planes = back_ref.shape[0] // SLOTS
+    lines = back_ref.shape[0]
     pos = pos_ref[...].astype(F32)
     order = sort_table(pos).astype(BF16)
     row = jnp.floor((pos + 0.5) * (1.0 / GRID))
@@ -423,11 +415,9 @@
     depth = jnp.where(depth < half, depth, depth - GRID)
     kinetic = (depth * depth + (row * row + col * col)) * (8.0 / (GRID * GRID))
     factor = kinetic - energy_ref[0]
-    real = back_ref[pl.ds(0, planes, stride=SLOTS), :]
-    imag = back_ref[pl.ds(1, planes, stride=SLOTS), :]
-    high, low = halves(jnp.concatenate([real, imag], axis=0))
+    high, low = halves(back_ref[...])
     both = dot(jnp.concatenate([high, low], axis=0), order).astype(BF16)
-    applied = dot(table[...], jnp.concatenate([both, both[: 2 * planes]], axis=0))
+    applied = dot(table[...], jnp.concatenate([both, both[:lines]], axis=0))
     for k in range(2):
         out_ref[k, 0] = factor * chg_ref[k, 0] + applied[k * GRID : (k + 1) * GRID]
     high, low = halves(parts[0][...] + parts[1][...] + parts[2][...] + parts[3][...])
@@ -477,6 +467,7 @@
     to_planes = np.block([[cos, -sin], [sin, cos]]) / math.sqrt(GRID)
     to_planes = np.stack(split_table(to_planes))
     from_planes = np.block([[cos.T, sin.T], [-sin.T, cos.T]]) / math.sqrt(planes)
+    from_planes = from_planes.reshape(2 * GRID, 2, planes).swapaxes(1, 2).reshape(2 * GRID, -1)
     high, low = split_table(from_planes)
     from_planes = np.concatenate([high, high, low], axis=1)
     right, left, left_back, right_back = transform_tables()
@@ -484,7 +475,7 @@
     pos = stick_pos.reshape(1, LANES)
     square = pltpu.VMEM((2 * PAD, 2 * PAD), BF16)
     grouped = pltpu.VMEM((CHUNKS * SLOTS, WIDE), F32)
-    windows = pltpu.SMEM((2 * CHUNKS,), jnp.int32)
+    windows = pltpu.SMEM((3 * CHUNKS,), jnp.int32)
 
     packed = call(
         planes_kernel,
@@ -504,41 +495,40 @@
     arrived = lax.all_to_all(
         packed.reshape(planes, SLOTS, LANES), "pw", split_axis=0, concat_axis=0, tiled=True
     ).reshape(planes * SLOTS, LANES)
-    pots = call(
+    pots, done = call(
         reorder_kernel,
         "reorder",
-        shape(2, PAD, PAD),
+        [shape(2, PAD, PAD), shape(1, dtype=jnp.int32)],
         in_vmem(3),
-        in_vmem(1)[0],
+        in_vmem(1) + [in_smem()],
         [pltpu.VMEM((3 * GRID, LANES), F32), pltpu.VMEM((PAD, PAD), F32)],
         flops=1_500_000_000,
         limit=60,
     )(potential, perturbation, order)
 
-    keep, send, h_high, h_low, group = call(
+    keep, send, fields, group = call(
         forward_kernel,
         "place_and_transform",
         [
             shape(4, 48, PAD),
             shape(4, 48, PAD),
-            shape(2 * PAD, PAD, dtype=BF16),
-            shape(2 * PAD, PAD, dtype=BF16),
+            shape(2 * PAD, 2 * PAD),
             shape(CHUNKS * SLOTS, WIDE),
         ],
-        in_vmem(6),
-        in_vmem(5),
+        [in_smem()] + in_vmem(5),
+        in_vmem(4),
         [windows, pltpu.VMEM((4, TALL, PAD), F32)]
         + [square] * 4
         + [pltpu.VMEM((3, LANES, PAD), F32)],
         flops=10_000_000_000,
-    )(arrived, pots, *right, *left)
+    )(done, arrived, *right, *left)
     got = lax.ppermute(send, "band", [(i, i ^ 1) for i in range(bands)])
-    picked = call(
+    picked, done = call(
         back_kernel,
         "back_and_pick",
-        shape(planes * SLOTS, LANES),
+        [shape(2 * planes, LANES), shape(1, dtype=jnp.int32)],
         in_vmem(7),
-        in_vmem(1)[0],
+        in_vmem(1) + [in_smem()],
         [
             pltpu.VMEM((2 * PAD, PAD), F32),
             pltpu.VMEM((PAD, 2 * PAD), BF16),
@@ -548,19 +538,17 @@
             windows,
         ],
         flops=6_000_000_000,
-    )(group, h_high, h_low, *left_back, *right_back)
-    returned = lax.all_to_all(
-        picked.reshape(planes, SLOTS, LANES), "pw", split_axis=0, concat_axis=0, tiled=True
-    ).reshape(planes * SLOTS, LANES)
+    )(group, fields, pots, *left_back, *right_back)
+    returned = lax.all_to_all(picked, "pw", split_axis=0, concat_axis=0, tiled=True)
     blocks = call(
         pair_kernel,
         "pair_sum",
         [shape(48, PAD)] * 4,
-        in_vmem(2),
+        [in_smem()] + in_vmem(2),
         in_vmem(4),
         [pltpu.VMEM((4, 48, PAD), F32)],
         flops=300_000,
-    )(keep, got)
+    )(done, keep, got)
     parts = [blocks[0]] + [
         lax.ppermute(blocks[k], "band", [(i, i ^ (2 * k)) for i in range(bands)])
         for k in range(1, 4)

time: 58 us -> 60.8 us (1.048)
  waiting for transfers between devices: 11 us -> 13.8 us
  local copies, waits for them, and re-layouts: 1.33 us -> 0.09 us
  Pallas kernels: 21.9 us -> 22.6 us
    all_to_all x1, waiting for transfers between devices: 5.12 us -> 7.98 us  [on_device(): lax.all_to_all(picked, 'pw', split_axis=0, concat_axis=0, tiled=True)]
    unnamed x26, local copies, waits for them, and re-layouts: 1.33 us -> 0.09 us
  transfers between devices with their start and end apart: 6 -> 6, of which waited for: 2 -> 2; matrix products, arithmetic and copies ran while one was open for 0% -> 0% of each run, Pallas kernels for 15% -> 14%
where the time goes in v2:
time: 60.8 us; the launch traced here: 60 us
  Pallas kernels  22.6 us (37%)
  starting transfers between devices  22 us (36%)
  waiting for transfers between devices  13.8 us (23%)
  between operations  1.5 us (2%)
    all_to_all x1, starting transfers between devices, on_device(): lax.all_to_all(packed.reshape(planes, SLOTS, LANES), 'pw', split_axis=0,...  11.9 us
    pallas_call x1, Pallas kernels, on_device(): call(forward_kernel, 'place_and_transform', [shape(4, 48, PAD), shape(4,...  9.76 us
    all_to_all x1, waiting for transfers between devices, on_device(): lax.all_to_all(picked, 'pw', split_axis=0, concat_axis=0, tiled=True)  7.98 us
    all_to_all x1, waiting for transfers between devices, on_device(): lax.all_to_all(packed.reshape(planes, SLOTS, LANES), 'pw', split_axis=0,...  5.84 us
    pallas_call x1, Pallas kernels, on_device(): call(back_kernel, 'back_and_pick', [shape(2 * planes, LANES), shape(1, dt...  4.91 us
    ppermute x3, starting transfers between devices, on_device(): lax.ppermute(blocks[k], 'band', [(i, i ^ 2 * k) for i in range(bands)])  4 us
    all_to_all x1, starting transfers between devices, on_device(): lax.all_to_all(picked, 'pw', split_axis=0, concat_axis=0, tiled=True)  3.85 us
    pallas_call x1, Pallas kernels, on_device(): call(reorder_kernel, 'reorder', [shape(2, PAD, PAD), shape(1, dtype=jnp.i...  3.45 us
  transfers between devices with their start and end apart: 6, of which 2 were waited for; matrix products, arithmetic and copies ran while one was open for 0% of the time, Pallas kernels for 14%

profile of v2, /device:TPU:1, one launch (start us, length us, event | category | flops | bytes accessed | tf_op | source)
XLA Modules:
  0.0 60.0 jit_solution(16697458250853381401)
XLA Ops:
  0.6 2.4 %to_planes.1 = f32[256,128]{1,0:T(8,128)} custom-call(s32[1,128]{1,0:T(1,128)} %bitcast.8, bf16[2,64,720]{2,1,0:T(8,128)(2,1)} %constant.22.clone.table_any, f32[2,1,360,128]{3,2,1,0:T(8,128)} %orb_any.1, f32[2,1,360,128]{3,2,1,0:T(8,128)} %chg_ref.1), custom_call_target="tpu_custom_call" | custom-call | flops 500000000 | bytes 3000000 | tf_op jit(solution)/shard_map/to_planes/pallas_call | solution.py:480
  3.0 11.9 %all-to-all-start = ((f32[32,8,128]{2,1,0:T(8,128)}), f32[32,8,128]{2,1,0:T(8,128)S(1)}, u32[]{:S(2)}, u32[]{:S(2)}) async-start(f32[32,8,128]{2,1,0:T(8,128)} %bitcast.10), calls=%async_computation | async-start | bytes 262144 | tf_op jit(solution)/shard_map/all_to_all | solution.py:495
  14.9 0.0 copy-start.6
  14.9 0.0 copy-start.7
  14.9 0.0 copy-start.8
  14.9 0.0 copy-start.9
  15.0 3.4 %reorder.1 = (f32[2,384,384]{2,1,0:T(8,128)}, s32[1]{0:T(128)}) custom-call(f32[1,360,360]{2,1,0:T(8,128)} %pot_ref.1, f32[1,360,360]{2,1,0:T(8,128)} %per_ref.1, bf16[384,384]{1,0:T(8,128)(2,1)} %constant.23.clone.order_ref), custom_call_target="tpu_custom_call" | custom-call | flops 1500000000 | bytes 3000000 | tf_op jit(solution)/shard_map/reorder/pallas_call | solution.py:498
  18.4 5.8 %all-to-all-done = f32[32,8,128]{2,1,0:T(8,128)S(1)} async-done(((f32[32,8,128]{2,1,0:T(8,128)}), f32[32,8,128]{2,1,0:T(8,128)S(1)}, u32[]{:S(2)}, u32[]{:S(2)}) %all-to-all-start) | async-done | bytes 131104 | tf_op jit(solution)/shard_map/all_to_all | solution.py:495
  24.3 0.0 copy-start.2
  24.3 0.0 copy-start.3
  24.3 0.0 copy-start.4
  24.3 0.0 copy-start.5
  24.3 9.8 %place_and_transform.1 = (f32[4,48,384]{2,1,0:T(8,128)S(1)}, f32[4,48,384]{2,1,0:T(8,128)S(1)}, f32[768,768]{1,0:T(8,128)S(1)}, f32[128,256]{1,0:T(8,128)S(1)}) custom-call(s32[1]{0:T(128)} %get-tuple-element.16.done_ref, f32[256,128]{1,0:T(8,128)S(1)} %bitcast.6, bf16[768,256]{1,0:T(8,128)(2,1)S(1)} %copy-done.6, bf16[768,256]{1,0:T(8,128)(2,1)S(1)} %copy-done.7, ...), custom_call_target="tpu_custom_call" | custom-call | flops 10000000000 | bytes 3000000 | tf_op jit(solution)/shard_map/place_and_transform/pallas_call | solution.py:509
  34.1 2.3 %collective-permute-start = (f32[4,48,384]{2,1,0:T(8,128)S(1)}, f32[4,48,384]{2,1,0:T(8,128)S(1)}, u32[]{:S(2)}, u32[]{:S(2)}) collective-permute-start(f32[4,48,384]{2,1,0:T(8,128)S(1)} %get-tuple-element.23), channel_id=1, source_target_pairs={{0,32},{32,0},{64,96},{96,64},{128,160},{160,128},{192,224},{224,1... | collective-permute-start | bytes 884744 | tf_op jit(solution)/shard_map/ppermute | solution.py:525
  36.4 0.0 copy-start
  36.5 0.0 copy-start.10
  36.5 0.0 copy-start.11
  36.5 4.9 %back_and_pick.1 = (f32[64,128]{1,0:T(8,128)}, s32[1]{0:T(128)}) custom-call(f32[128,256]{1,0:T(8,128)S(1)} %get-tuple-element.17.group_ref, f32[768,768]{1,0:T(8,128)S(1)} %get-tuple-element.18.real_ref, f32[2,384,384]{2,1,0:T(8,128)S(1)} %copy-done.12, bf16[768,256]{1,0:T(8,128)(2,1)S(1)} %copy-done.2, bf16[768,256]{1,0:T(8,128)(2,1)S(1)} %copy-done.3, ...), custom_call_target="tpu_custom_call" | custom-call | flops 6000000000 | bytes 3000000 | tf_op jit(solution)/shard_map/back_and_pick/pallas_call | solution.py:526
  41.4 0.7 %pair_sum.1 = (f32[48,384]{1,0:T(8,128)S(1)}, f32[48,384]{1,0:T(8,128)S(1)}, f32[48,384]{1,0:T(8,128)S(1)}, f32[48,384]{1,0:T(8,128)S(1)}) custom-call(s32[1]{0:T(128)} %get-tuple-element.21.done_ref, f32[4,48,384]{2,1,0:T(8,128)S(1)} %get-tuple-element.22.keep_ref, f32[4,48,384]{2,1,0:T(8,128)S(1)} %collective-permute-done.got_ref), custom_call_target="tpu_custom_call" | custom-call | flops 300000 | bytes 3000000 | tf_op jit(solution)/shard_map/pair_sum/pallas_call | solution.py:543
  42.1 1.4 %collective-permute-start.1 = (f32[48,384]{1,0:T(8,128)S(1)}, f32[48,384]{1,0:T(8,128)S(1)}, u32[]{:S(2)}, u32[]{:S(2)}) collective-permute-start(f32[48,384]{1,0:T(8,128)S(1)} %get-tuple-element.25), channel_id=1, source_target_pairs={{0,64},{32,96},{64,0},{96,32},{128,192},{160,224},{192,128},{224,1... | collective-permute-start | bytes 221192 | tf_op jit(solution)/shard_map/ppermute | solution.py:553
  43.5 2.6 %collective-permute-start.2 = (f32[48,384]{1,0:T(8,128)S(1)}, f32[48,384]{1,0:T(8,128)S(1)}, u32[]{:S(2)}, u32[]{:S(2)}) collective-permute-start(f32[48,384]{1,0:T(8,128)S(1)} %get-tuple-element.26), channel_id=1, source_target_pairs={{0,128},{32,160},{64,192},{96,224},{128,0},{160,32},{192,64},{224,... | collective-permute-start | bytes 221192 | tf_op jit(solution)/shard_map/ppermute | solution.py:553
  46.1 3.9 %all-to-all-start.1 = ((f32[32,2,128]{2,1,0:T(2,128)}), f32[32,2,128]{2,1,0:T(2,128)S(1)}, u32[]{:S(2)}, u32[]{:S(2)}) async-start(f32[32,2,128]{2,1,0:T(2,128)} %bitcast.3), calls=%async_computation.1 | async-start | bytes 65536 | tf_op jit(solution)/shard_map/all_to_all | solution.py:542
  50.6 8.0 %all-to-all-done.1 = f32[32,2,128]{2,1,0:T(2,128)S(1)} async-done(((f32[32,2,128]{2,1,0:T(2,128)}), f32[32,2,128]{2,1,0:T(2,128)S(1)}, u32[]{:S(2)}, u32[]{:S(2)}) %all-to-all-start.1) | async-done | bytes 32800 | tf_op jit(solution)/shard_map/all_to_all | solution.py:542
  58.7 1.3 %from_planes.1 = (f32[2,1,360,128]{3,2,1,0:T(8,128)}, f32[45,1,360]{2,1,0:T(1,128)}) custom-call(s32[1,128]{1,0:T(1,128)S(1)} %bitcast.9, bf16[720,192]{1,0:T(8,128)(2,1)S(1)} %copy-done.10, bf16[384,384]{1,0:T(8,128)(2,1)S(1)} %copy-done.11, f32[2,1,360,128]{3,2,1,0:T(8,128)S(1)} %copy-done, f32[64,128]{1,0:T(8,128)S(1)} %bitcast.7, f32[1]{0:T(128)S(6)} %copy.19.energy_ref, ...), custom_call_target="tpu_custom_call" | custom-call | flops 500000000 | bytes 3000000 | tf_op jit(solution)/shard_map/from_planes/pallas_call | solution.py:557
  (20 shorter events, 0.0 us)
Async XLA Ops:
  3.0 21.2 %all-to-all-start = ((f32[32,8,128]{2,1,0:T(8,128)}), f32[32,8,128]{2,1,0:T(8,128)S(1)}, u32[]{:S(2)}, u32[]{:S(2)}) async-start(f32[32,8,128]{2,1,0:T(8,128)} %bitcast.10), calls=%async_computation | async-start | bytes 262144 | tf_op jit(solution)/shard_map/all_to_all | solution.py:495
  14.9 9.3 %copy-start.6 = (bf16[768,256]{1,0:T(8,128)(2,1)S(1)}, bf16[768,256]{1,0:T(8,128)(2,1)}, u32[]{:S(2)}) copy-start(bf16[768,256]{1,0:T(8,128)(2,1)} %constant.24.clone.rh_ref) | copy-start | bytes 1179652
  14.9 9.3 %copy-start.7 = (bf16[768,256]{1,0:T(8,128)(2,1)S(1)}, bf16[768,256]{1,0:T(8,128)(2,1)}, u32[]{:S(2)}) copy-start(bf16[768,256]{1,0:T(8,128)(2,1)} %constant.25.clone.rl_ref) | copy-start | bytes 1179652
  14.9 9.3 %copy-start.8 = (bf16[768,256]{1,0:T(8,128)(2,1)S(1)}, bf16[768,256]{1,0:T(8,128)(2,1)}, u32[]{:S(2)}) copy-start(bf16[768,256]{1,0:T(8,128)(2,1)} %constant.26.clone.lh_ref) | copy-start | bytes 1179652
  14.9 9.3 %copy-start.9 = (bf16[768,256]{1,0:T(8,128)(2,1)S(1)}, bf16[768,256]{1,0:T(8,128)(2,1)}, u32[]{:S(2)}) copy-start(bf16[768,256]{1,0:T(8,128)(2,1)} %constant.27.clone.ll_ref) | copy-start | bytes 1179652
  24.3 12.1 %copy-start.2 = (bf16[768,256]{1,0:T(8,128)(2,1)S(1)}, bf16[768,256]{1,0:T(8,128)(2,1)}, u32[]{:S(2)}) copy-start(bf16[768,256]{1,0:T(8,128)(2,1)} %constant.28.clone.lh_ref) | copy-start | bytes 1179652
  24.3 12.1 %copy-start.3 = (bf16[768,256]{1,0:T(8,128)(2,1)S(1)}, bf16[768,256]{1,0:T(8,128)(2,1)}, u32[]{:S(2)}) copy-start(bf16[768,256]{1,0:T(8,128)(2,1)} %constant.29.clone.ll_ref) | copy-start | bytes 1179652
  24.3 12.1 %copy-start.4 = (bf16[768,256]{1,0:T(8,128)(2,1)S(1)}, bf16[768,256]{1,0:T(8,128)(2,1)}, u32[]{:S(2)}) copy-start(bf16[768,256]{1,0:T(8,128)(2,1)} %constant.30.clone.rh_ref) | copy-start | bytes 1179652
  24.3 12.1 %copy-start.5 = (bf16[768,256]{1,0:T(8,128)(2,1)S(1)}, bf16[768,256]{1,0:T(8,128)(2,1)}, u32[]{:S(2)}) copy-start(bf16[768,256]{1,0:T(8,128)(2,1)} %constant.31.clone.rl_ref) | copy-start | bytes 1179652
  24.3 12.1 %copy-start.12 = (f32[2,384,384]{2,1,0:T(8,128)S(1)}, f32[2,384,384]{2,1,0:T(8,128)}, u32[]{:S(2)}) copy-start(f32[2,384,384]{2,1,0:T(8,128)} %get-tuple-element.19.pot_ref) | copy-start | bytes 3538948
  34.1 7.3 %collective-permute-start = (f32[4,48,384]{2,1,0:T(8,128)S(1)}, f32[4,48,384]{2,1,0:T(8,128)S(1)}, u32[]{:S(2)}, u32[]{:S(2)}) collective-permute-start(f32[4,48,384]{2,1,0:T(8,128)S(1)} %get-tuple-element.23), channel_id=1, source_target_pairs={{0,32},{32,0},{64,96},{96,64},{128,160},{160,128},{192,224},{224,1... | collective-permute-start | bytes 884744 | tf_op jit(solution)/shard_map/ppermute | solution.py:525
  36.4 22.2 %copy-start = (f32[2,1,360,128]{3,2,1,0:T(8,128)S(1)}, f32[2,1,360,128]{3,2,1,0:T(8,128)}, u32[]{:S(2)}) copy-start(f32[2,1,360,128]{3,2,1,0:T(8,128)} %chg_ref.1) | copy-start | bytes 1105924
  36.5 22.2 %copy-start.1 = (s32[128]{0:T(128)S(1)}, s32[128]{0:T(128)}, u32[]{:S(2)}) copy-start(s32[128]{0:T(128)} %param.22) | copy-start | bytes 1540
  36.5 22.2 %copy-start.10 = (bf16[720,192]{1,0:T(8,128)(2,1)S(1)}, bf16[720,192]{1,0:T(8,128)(2,1)}, u32[]{:S(2)}) copy-start(bf16[720,192]{1,0:T(8,128)(2,1)} %constant.32.clone.table) | copy-start | bytes 829444
  36.5 22.2 %copy-start.11 = (bf16[384,384]{1,0:T(8,128)(2,1)S(1)}, bf16[384,384]{1,0:T(8,128)(2,1)}, u32[]{:S(2)}) copy-start(bf16[384,384]{1,0:T(8,128)(2,1)} %constant.23.clone.order_ref) | copy-start | bytes 884740
  42.1 16.5 %collective-permute-start.1 = (f32[48,384]{1,0:T(8,128)S(1)}, f32[48,384]{1,0:T(8,128)S(1)}, u32[]{:S(2)}, u32[]{:S(2)}) collective-permute-start(f32[48,384]{1,0:T(8,128)S(1)} %get-tuple-element.25), channel_id=1, source_target_pairs={{0,64},{32,96},{64,0},{96,32},{128,192},{160,224},{192,128},{224,1... | collective-permute-start | bytes 221192 | tf_op jit(solution)/shard_map/ppermute | solution.py:553
  43.5 15.1 %collective-permute-start.2 = (f32[48,384]{1,0:T(8,128)S(1)}, f32[48,384]{1,0:T(8,128)S(1)}, u32[]{:S(2)}, u32[]{:S(2)}) collective-permute-start(f32[48,384]{1,0:T(8,128)S(1)} %get-tuple-element.26), channel_id=1, source_target_pairs={{0,128},{32,160},{64,192},{96,224},{128,0},{160,32},{192,64},{224,... | collective-permute-start | bytes 221192 | tf_op jit(solution)/shard_map/ppermute | solution.py:553
  46.1 12.5 %collective-permute-start.3 = (f32[48,384]{1,0:T(8,128)S(1)}, f32[48,384]{1,0:T(8,128)S(1)}, u32[]{:S(2)}, u32[]{:S(2)}) collective-permute-start(f32[48,384]{1,0:T(8,128)S(1)} %get-tuple-element.27), channel_id=1, source_target_pairs={{0,192},{32,224},{64,128},{96,160},{128,64},{160,96},{192,0},{224,... | collective-permute-start | bytes 221192 | tf_op jit(solution)/shard_map/ppermute | solution.py:553
  46.1 12.5 %all-to-all-start.1 = ((f32[32,2,128]{2,1,0:T(2,128)}), f32[32,2,128]{2,1,0:T(2,128)S(1)}, u32[]{:S(2)}, u32[]{:S(2)}) async-start(f32[32,2,128]{2,1,0:T(2,128)} %bitcast.3), calls=%async_computation.1 | async-start | bytes 65536 | tf_op jit(solution)/shard_map/all_to_all | solution.py:542

commit v3 on v2

--- a/solution.py
+++ b/solution.py
@@ -388,7 +388,7 @@
         ]
         for j, block in enumerate(exchange_lanes(blocks)):
             src = half * CHUNKS + j
-            out_ref[2 * src : 2 * src + 2, :] = block[0:2, :]
+            out_ref[src * SLOTS : (src + 1) * SLOTS, :] = block
 
 
 def pair_kernel(done_ref, keep_ref, got_ref, *rest):
@@ -403,7 +403,8 @@
     pos_ref, table, order_ref, chg_ref, back_ref, energy_ref, *rest
 ):
     parts, (out_ref, dens_ref) = rest[:4], rest[4:]
-    lines = back_ref.shape[0]
+    planes = back_ref.shape[0] // SLOTS
+    lines = 2 * planes
     pos = pos_ref[...].astype(F32)
     order = sort_table(pos).astype(BF16)
     row = jnp.floor((pos + 0.5) * (1.0 / GRID))
@@ -415,7 +416,9 @@
     depth = jnp.where(depth < half, depth, depth - GRID)
     kinetic = (depth * depth + (row * row + col * col)) * (8.0 / (GRID * GRID))
     factor = kinetic - energy_ref[0]
-    high, low = halves(back_ref[...])
+    real = back_ref[pl.ds(0, planes, stride=SLOTS), :]
+    imag = back_ref[pl.ds(1, planes, stride=SLOTS), :]
+    high, low = halves(jnp.concatenate([real, imag], axis=0))
     both = dot(jnp.concatenate([high, low], axis=0), order).astype(BF16)
     applied = dot(table[...], jnp.concatenate([both, both[:lines]], axis=0))
     for k in range(2):
@@ -467,7 +470,6 @@
     to_planes = np.block([[cos, -sin], [sin, cos]]) / math.sqrt(GRID)
     to_planes = np.stack(split_table(to_planes))
     from_planes = np.block([[cos.T, sin.T], [-sin.T, cos.T]]) / math.sqrt(planes)
-    from_planes = from_planes.reshape(2 * GRID, 2, planes).swapaxes(1, 2).reshape(2 * GRID, -1)
     high, low = split_table(from_planes)
     from_planes = np.concatenate([high, high, low], axis=1)
     right, left, left_back, right_back = transform_tables()
@@ -526,7 +528,7 @@
     picked, done = call(
         back_kernel,
         "back_and_pick",
-        [shape(2 * planes, LANES), shape(1, dtype=jnp.int32)],
+        [shape(planes * SLOTS, LANES), shape(1, dtype=jnp.int32)],
         in_vmem(7),
         in_vmem(1) + [in_smem()],
         [
@@ -539,7 +541,9 @@
         ],
         flops=6_000_000_000,
     )(group, fields, pots, *left_back, *right_back)
-    returned = lax.all_to_all(picked, "pw", split_axis=0, concat_axis=0, tiled=True)
+    returned = lax.all_to_all(
+        picked.reshape(planes, SLOTS, LANES), "pw", split_axis=0, concat_axis=0, tiled=True
+    ).reshape(planes * SLOTS, LANES)
     blocks = call(
         pair_kernel,
         "pair_sum",

time: 60.8 us -> 57.1 us (0.939)
  waiting for transfers between devices: 13.8 us -> 10.6 us
    all_to_all x1, waiting for transfers between devices: 7.98 us -> 4.49 us  [on_device(): lax.all_to_all(picked.reshape(planes, SLOTS, LANES), 'pw', split_axis=0,...]
  transfers between devices with their start and end apart: 6 -> 6, of which waited for: 2 -> 3; matrix products, arithmetic and copies ran while one was open for 0% -> 0% of each run, Pallas kernels for 14% -> 16%
where the time goes in v3:
time: 57.1 us; the launch traced here: 56.8 us
  Pallas kernels  22.6 us (40%)
  starting transfers between devices  22.1 us (39%)
  waiting for transfers between devices  10.6 us (19%)
  between operations  1.48 us (3%)
    all_to_all x1, starting transfers between devices, on_device(): lax.all_to_all(packed.reshape(planes, SLOTS, LANES), 'pw', split_axis=0,...  11.9 us
    pallas_call x1, Pallas kernels, on_device(): call(forward_kernel, 'place_and_transform', [shape(4, 48, PAD), shape(4,...  9.73 us
    all_to_all x1, waiting for transfers between devices, on_device(): lax.all_to_all(packed.reshape(planes, SLOTS, LANES), 'pw', split_axis=0,...  5.84 us
    pallas_call x1, Pallas kernels, on_device(): call(back_kernel, 'back_and_pick', [shape(planes * SLOTS, LANES), shape(1...  4.94 us
    all_to_all x1, waiting for transfers between devices, on_device(): lax.all_to_all(picked.reshape(planes, SLOTS, LANES), 'pw', split_axis=0,...  4.49 us
    ppermute x3, starting transfers between devices, on_device(): lax.ppermute(blocks[k], 'band', [(i, i ^ 2 * k) for i in range(bands)])  4 us
    all_to_all x1, starting transfers between devices, on_device(): lax.all_to_all(picked.reshape(planes, SLOTS, LANES), 'pw', split_axis=0,...  3.87 us
    pallas_call x1, Pallas kernels, on_device(): call(reorder_kernel, 'reorder', [shape(2, PAD, PAD), shape(1, dtype=jnp.i...  3.45 us
  transfers between devices with their start and end apart: 6, of which 3 were waited for; matrix products, arithmetic and copies ran while one was open for 0% of the time, Pallas kernels for 16%

profile of v3, /device:TPU:1, one launch (start us, length us, event | category | flops | bytes accessed | tf_op | source)
XLA Modules:
  0.0 56.8 jit_solution(16062390600011218559)
XLA Ops:
  0.6 2.4 %to_planes.1 = f32[256,128]{1,0:T(8,128)} custom-call(s32[1,128]{1,0:T(1,128)} %bitcast.8, bf16[2,64,720]{2,1,0:T(8,128)(2,1)} %constant.22.clone.table_any, f32[2,1,360,128]{3,2,1,0:T(8,128)} %orb_any.1, f32[2,1,360,128]{3,2,1,0:T(8,128)} %chg_ref.1), custom_call_target="tpu_custom_call" | custom-call | flops 500000000 | bytes 3000000 | tf_op jit(solution)/shard_map/to_planes/pallas_call | solution.py:482
  3.0 11.9 %all-to-all-start = ((f32[32,8,128]{2,1,0:T(8,128)}), f32[32,8,128]{2,1,0:T(8,128)S(1)}, u32[]{:S(2)}, u32[]{:S(2)}) async-start(f32[32,8,128]{2,1,0:T(8,128)} %bitcast.10), calls=%async_computation | async-start | bytes 262144 | tf_op jit(solution)/shard_map/all_to_all | solution.py:497
  14.9 0.0 copy-start.6
  14.9 0.0 copy-start.7
  14.9 0.0 copy-start.8
  14.9 0.0 copy-start.9
  15.0 3.4 %reorder.1 = (f32[2,384,384]{2,1,0:T(8,128)}, s32[1]{0:T(128)}) custom-call(f32[1,360,360]{2,1,0:T(8,128)} %pot_ref.1, f32[1,360,360]{2,1,0:T(8,128)} %per_ref.1, bf16[384,384]{1,0:T(8,128)(2,1)} %constant.23.clone.order_ref), custom_call_target="tpu_custom_call" | custom-call | flops 1500000000 | bytes 3000000 | tf_op jit(solution)/shard_map/reorder/pallas_call | solution.py:500
  18.4 5.8 %all-to-all-done = f32[32,8,128]{2,1,0:T(8,128)S(1)} async-done(((f32[32,8,128]{2,1,0:T(8,128)}), f32[32,8,128]{2,1,0:T(8,128)S(1)}, u32[]{:S(2)}, u32[]{:S(2)}) %all-to-all-start) | async-done | bytes 131104 | tf_op jit(solution)/shard_map/all_to_all | solution.py:497
  24.3 0.0 copy-start.2
  24.3 0.0 copy-start.3
  24.3 0.0 copy-start.4
  24.3 0.0 copy-start.5
  24.3 9.7 %place_and_transform.1 = (f32[4,48,384]{2,1,0:T(8,128)S(1)}, f32[4,48,384]{2,1,0:T(8,128)S(1)}, f32[768,768]{1,0:T(8,128)S(1)}, f32[128,256]{1,0:T(8,128)S(1)}) custom-call(s32[1]{0:T(128)} %get-tuple-element.16.done_ref, f32[256,128]{1,0:T(8,128)S(1)} %bitcast.7, bf16[768,256]{1,0:T(8,128)(2,1)S(1)} %copy-done.6, bf16[768,256]{1,0:T(8,128)(2,1)S(1)} %copy-done.7, ...), custom_call_target="tpu_custom_call" | custom-call | flops 10000000000 | bytes 3000000 | tf_op jit(solution)/shard_map/place_and_transform/pallas_call | solution.py:511
  34.1 2.3 %collective-permute-start = (f32[4,48,384]{2,1,0:T(8,128)S(1)}, f32[4,48,384]{2,1,0:T(8,128)S(1)}, u32[]{:S(2)}, u32[]{:S(2)}) collective-permute-start(f32[4,48,384]{2,1,0:T(8,128)S(1)} %get-tuple-element.23), channel_id=1, source_target_pairs={{0,32},{32,0},{64,96},{96,64},{128,160},{160,128},{192,224},{224,1... | collective-permute-start | bytes 884744 | tf_op jit(solution)/shard_map/ppermute | solution.py:527
  36.5 0.0 copy-start.10
  36.5 0.0 copy-start.11
  36.5 4.9 %back_and_pick.1 = (f32[256,128]{1,0:T(8,128)}, s32[1]{0:T(128)}) custom-call(f32[128,256]{1,0:T(8,128)S(1)} %get-tuple-element.17.group_ref, f32[768,768]{1,0:T(8,128)S(1)} %get-tuple-element.18.real_ref, f32[2,384,384]{2,1,0:T(8,128)S(1)} %copy-done.12, bf16[768,256]{1,0:T(8,128)(2,1)S(1)} %copy-done.2, bf16[768,256]{1,0:T(8,128)(2,1)S(1)} %copy-done.3, ...), custom_call_target="tpu_custom_call" | custom-call | flops 6000000000 | bytes 3000000 | tf_op jit(solution)/shard_map/back_and_pick/pallas_call | solution.py:528
  41.4 3.9 %all-to-all-start.1 = ((f32[32,8,128]{2,1,0:T(8,128)}), f32[32,8,128]{2,1,0:T(8,128)S(1)}, u32[]{:S(2)}, u32[]{:S(2)}) async-start(f32[32,8,128]{2,1,0:T(8,128)} %bitcast.3), calls=%async_computation.1 | async-start | bytes 262144 | tf_op jit(solution)/shard_map/all_to_all | solution.py:544
  45.3 0.7 %pair_sum.1 = (f32[48,384]{1,0:T(8,128)S(1)}, f32[48,384]{1,0:T(8,128)S(1)}, f32[48,384]{1,0:T(8,128)S(1)}, f32[48,384]{1,0:T(8,128)S(1)}) custom-call(s32[1]{0:T(128)} %get-tuple-element.21.done_ref, f32[4,48,384]{2,1,0:T(8,128)S(1)} %get-tuple-element.22.keep_ref, f32[4,48,384]{2,1,0:T(8,128)S(1)} %collective-permute-done.got_ref), custom_call_target="tpu_custom_call" | custom-call | flops 300000 | bytes 3000000 | tf_op jit(solution)/shard_map/pair_sum/pallas_call | solution.py:547
  46.0 1.4 %collective-permute-start.1 = (f32[48,384]{1,0:T(8,128)S(1)}, f32[48,384]{1,0:T(8,128)S(1)}, u32[]{:S(2)}, u32[]{:S(2)}) collective-permute-start(f32[48,384]{1,0:T(8,128)S(1)} %get-tuple-element.25), channel_id=1, source_target_pairs={{0,64},{32,96},{64,0},{96,32},{128,192},{160,224},{192,128},{224,1... | collective-permute-start | bytes 221192 | tf_op jit(solution)/shard_map/ppermute | solution.py:557
  47.4 2.6 %collective-permute-start.2 = (f32[48,384]{1,0:T(8,128)S(1)}, f32[48,384]{1,0:T(8,128)S(1)}, u32[]{:S(2)}, u32[]{:S(2)}) collective-permute-start(f32[48,384]{1,0:T(8,128)S(1)} %get-tuple-element.26), channel_id=1, source_target_pairs={{0,128},{32,160},{64,192},{96,224},{128,0},{160,32},{192,64},{224,... | collective-permute-start | bytes 221192 | tf_op jit(solution)/shard_map/ppermute | solution.py:557
  50.7 4.5 %all-to-all-done.1 = f32[32,8,128]{2,1,0:T(8,128)S(1)} async-done(((f32[32,8,128]{2,1,0:T(8,128)}), f32[32,8,128]{2,1,0:T(8,128)S(1)}, u32[]{:S(2)}, u32[]{:S(2)}) %all-to-all-start.1) | async-done | bytes 131104 | tf_op jit(solution)/shard_map/all_to_all | solution.py:544
  55.2 0.2 collective-permute-done.3.rest_3_
  55.4 1.4 %from_planes.1 = (f32[2,1,360,128]{3,2,1,0:T(8,128)}, f32[45,1,360]{2,1,0:T(1,128)}) custom-call(s32[1,128]{1,0:T(1,128)S(1)} %bitcast.9, bf16[720,192]{1,0:T(8,128)(2,1)S(1)} %copy-done.10, bf16[384,384]{1,0:T(8,128)(2,1)S(1)} %copy-done.11, f32[2,1,360,128]{3,2,1,0:T(8,128)S(1)} %copy-done, f32[256,128]{1,0:T(8,128)S(1)} %bitcast.6, ...), custom_call_target="tpu_custom_call" | custom-call | flops 500000000 | bytes 3000000 | tf_op jit(solution)/shard_map/from_planes/pallas_call | solution.py:561
  (20 shorter events, 0.0 us)
Async XLA Ops:
  3.0 21.2 %all-to-all-start = ((f32[32,8,128]{2,1,0:T(8,128)}), f32[32,8,128]{2,1,0:T(8,128)S(1)}, u32[]{:S(2)}, u32[]{:S(2)}) async-start(f32[32,8,128]{2,1,0:T(8,128)} %bitcast.10), calls=%async_computation | async-start | bytes 262144 | tf_op jit(solution)/shard_map/all_to_all | solution.py:497
  14.9 9.3 %copy-start.6 = (bf16[768,256]{1,0:T(8,128)(2,1)S(1)}, bf16[768,256]{1,0:T(8,128)(2,1)}, u32[]{:S(2)}) copy-start(bf16[768,256]{1,0:T(8,128)(2,1)} %constant.24.clone.rh_ref) | copy-start | bytes 1179652
  14.9 9.3 %copy-start.7 = (bf16[768,256]{1,0:T(8,128)(2,1)S(1)}, bf16[768,256]{1,0:T(8,128)(2,1)}, u32[]{:S(2)}) copy-start(bf16[768,256]{1,0:T(8,128)(2,1)} %constant.25.clone.rl_ref) | copy-start | bytes 1179652
  14.9 9.3 %copy-start.8 = (bf16[768,256]{1,0:T(8,128)(2,1)S(1)}, bf16[768,256]{1,0:T(8,128)(2,1)}, u32[]{:S(2)}) copy-start(bf16[768,256]{1,0:T(8,128)(2,1)} %constant.26.clone.lh_ref) | copy-start | bytes 1179652
  14.9 9.3 %copy-start.9 = (bf16[768,256]{1,0:T(8,128)(2,1)S(1)}, bf16[768,256]{1,0:T(8,128)(2,1)}, u32[]{:S(2)}) copy-start(bf16[768,256]{1,0:T(8,128)(2,1)} %constant.27.clone.ll_ref) | copy-start | bytes 1179652
  24.3 12.1 %copy-start.2 = (bf16[768,256]{1,0:T(8,128)(2,1)S(1)}, bf16[768,256]{1,0:T(8,128)(2,1)}, u32[]{:S(2)}) copy-start(bf16[768,256]{1,0:T(8,128)(2,1)} %constant.28.clone.lh_ref) | copy-start | bytes 1179652
  24.3 12.1 %copy-start.3 = (bf16[768,256]{1,0:T(8,128)(2,1)S(1)}, bf16[768,256]{1,0:T(8,128)(2,1)}, u32[]{:S(2)}) copy-start(bf16[768,256]{1,0:T(8,128)(2,1)} %constant.29.clone.ll_ref) | copy-start | bytes 1179652
  24.3 12.1 %copy-start.4 = (bf16[768,256]{1,0:T(8,128)(2,1)S(1)}, bf16[768,256]{1,0:T(8,128)(2,1)}, u32[]{:S(2)}) copy-start(bf16[768,256]{1,0:T(8,128)(2,1)} %constant.30.clone.rh_ref) | copy-start | bytes 1179652
  24.3 12.1 %copy-start.5 = (bf16[768,256]{1,0:T(8,128)(2,1)S(1)}, bf16[768,256]{1,0:T(8,128)(2,1)}, u32[]{:S(2)}) copy-start(bf16[768,256]{1,0:T(8,128)(2,1)} %constant.31.clone.rl_ref) | copy-start | bytes 1179652
  24.3 12.1 %copy-start.12 = (f32[2,384,384]{2,1,0:T(8,128)S(1)}, f32[2,384,384]{2,1,0:T(8,128)}, u32[]{:S(2)}) copy-start(f32[2,384,384]{2,1,0:T(8,128)} %get-tuple-element.19.pot_ref) | copy-start | bytes 3538948
  34.1 11.2 %collective-permute-start = (f32[4,48,384]{2,1,0:T(8,128)S(1)}, f32[4,48,384]{2,1,0:T(8,128)S(1)}, u32[]{:S(2)}, u32[]{:S(2)}) collective-permute-start(f32[4,48,384]{2,1,0:T(8,128)S(1)} %get-tuple-element.23), channel_id=1, source_target_pairs={{0,32},{32,0},{64,96},{96,64},{128,160},{160,128},{192,224},{224,1... | collective-permute-start | bytes 884744 | tf_op jit(solution)/shard_map/ppermute | solution.py:527
  36.4 19.0 %copy-start = (f32[2,1,360,128]{3,2,1,0:T(8,128)S(1)}, f32[2,1,360,128]{3,2,1,0:T(8,128)}, u32[]{:S(2)}) copy-start(f32[2,1,360,128]{3,2,1,0:T(8,128)} %chg_ref.1) | copy-start | bytes 1105924
  36.4 19.0 %copy-start.1 = (s32[128]{0:T(128)S(1)}, s32[128]{0:T(128)}, u32[]{:S(2)}) copy-start(s32[128]{0:T(128)} %param.22) | copy-start | bytes 1540
  36.5 19.0 %copy-start.10 = (bf16[720,192]{1,0:T(8,128)(2,1)S(1)}, bf16[720,192]{1,0:T(8,128)(2,1)}, u32[]{:S(2)}) copy-start(bf16[720,192]{1,0:T(8,128)(2,1)} %constant.32.clone.table) | copy-start | bytes 829444
  36.5 19.0 %copy-start.11 = (bf16[384,384]{1,0:T(8,128)(2,1)S(1)}, bf16[384,384]{1,0:T(8,128)(2,1)}, u32[]{:S(2)}) copy-start(bf16[384,384]{1,0:T(8,128)(2,1)} %constant.23.clone.order_ref) | copy-start | bytes 884740
  41.4 13.7 %all-to-all-start.1 = ((f32[32,8,128]{2,1,0:T(8,128)}), f32[32,8,128]{2,1,0:T(8,128)S(1)}, u32[]{:S(2)}, u32[]{:S(2)}) async-start(f32[32,8,128]{2,1,0:T(8,128)} %bitcast.3), calls=%async_computation.1 | async-start | bytes 262144 | tf_op jit(solution)/shard_map/all_to_all | solution.py:544
  46.0 9.2 %collective-permute-start.1 = (f32[48,384]{1,0:T(8,128)S(1)}, f32[48,384]{1,0:T(8,128)S(1)}, u32[]{:S(2)}, u32[]{:S(2)}) collective-permute-start(f32[48,384]{1,0:T(8,128)S(1)} %get-tuple-element.25), channel_id=1, source_target_pairs={{0,64},{32,96},{64,0},{96,32},{128,192},{160,224},{192,128},{224,1... | collective-permute-start | bytes 221192 | tf_op jit(solution)/shard_map/ppermute | solution.py:557
  47.4 7.8 %collective-permute-start.2 = (f32[48,384]{1,0:T(8,128)S(1)}, f32[48,384]{1,0:T(8,128)S(1)}, u32[]{:S(2)}, u32[]{:S(2)}) collective-permute-start(f32[48,384]{1,0:T(8,128)S(1)} %get-tuple-element.26), channel_id=1, source_target_pairs={{0,128},{32,160},{64,192},{96,224},{128,0},{160,32},{192,64},{224,... | collective-permute-start | bytes 221192 | tf_op jit(solution)/shard_map/ppermute | solution.py:557
  50.0 5.4 %collective-permute-start.3 = (f32[48,384]{1,0:T(8,128)S(1)}, f32[48,384]{1,0:T(8,128)S(1)}, u32[]{:S(2)}, u32[]{:S(2)}) collective-permute-start(f32[48,384]{1,0:T(8,128)S(1)} %get-tuple-element.27), channel_id=1, source_target_pairs={{0,192},{32,224},{64,128},{96,160},{128,64},{160,96},{192,0},{224,... | collective-permute-start | bytes 221192 | tf_op jit(solution)/shard_map/ppermute | solution.py:557
